TPU v7x, 32 devices: a whole 2x2x4 slice. The times are simulated.
32 devices in a mesh: grp: 1, kz: 32 (over z, y, x, core).
Axes of the slice: x: 2, y: 2, z: 4, core: 2. Of those that a mesh axis runs over, the one named last changes fastest.
Arguments:
- kspace: float32 [8, 16, 512, 512], P('grp', None, 'kz'), may hold values from -8 to 8
- sensitivity: float32 [2, 256, 8, 16, 512], P(None, ('grp', 'kz')), may hold values from -2 to 2
- weight_first: bfloat16 [24, 2, 3, 3, 3], replicated, may hold values from -0.875 to 0.875
- bias_first: float32 [24], replicated, may hold values from -0.5 to 0.5
- weight_second: bfloat16 [24, 24, 3, 3, 3], replicated, may hold values from -0.3125 to 0.3125
- bias_second: float32 [24], replicated, may hold values from -0.5 to 0.5
- weight_third: bfloat16 [24, 24, 3, 3, 3], replicated, may hold values from -0.3125 to 0.3125
- bias_third: float32 [24], replicated, may hold values from -0.5 to 0.5
Outputs:
- features: bfloat16 [24, 512, 16, 256], P('grp', 'kz')
All inputs are finite; a program needn't handle non-finite values.
Results may differ from a plain program's by a relative error of at most 0.0058.
Values may be sent and summed in bfloat16 or wider, within the bound.
No kernel may reach another device: no remote copies, remote signals or barrier semaphores. Data moves between devices by JAX's collectives and lax.ppermute only.
A program may use at most 192 MiB of HBM per device.

v0:
```python
import math

import jax
import jax.numpy as jnp
from jax import lax
from jax.sharding import PartitionSpec as P

HIGHEST_PRECISION = lax.Precision.HIGHEST


def padded(x, sides, width):
    for axis, dim in sides:
        peers, length = (lax.axis_size(axis), x.shape[dim])
        up = [(i, (i + 1) % peers) for i in range(peers - 1)]
        down = [(j, i) for i, j in up]
        last = lax.slice_in_dim(x, length - width, length, axis=dim)
        first = lax.slice_in_dim(x, 0, width, axis=dim)
        before = lax.ppermute(last, axis, up)
        after = lax.ppermute(first, axis, down)
        x = jnp.concatenate([before, x, after], axis=dim)
    return x


def dft_parts(length):
    positions = jnp.arange(length, dtype=jnp.int32)
    phase_int = positions[:, None] * positions[None, :] % length
    angles = phase_int.astype(jnp.float32) * (2.0 * math.pi / length)
    factor = 1.0 / math.sqrt(length)
    return (jnp.cos(angles) * factor, jnp.sin(angles) * factor)


def y_table(length):
    cosine, sine_part = dft_parts(length)
    upper = jnp.concatenate([cosine, sine_part], axis=1)
    lower = jnp.concatenate([-sine_part, cosine], axis=1)
    return jnp.concatenate([upper, lower], axis=0)


def z_stacked(length):
    cosine, sine_part = dft_parts(length)
    from_real = jnp.stack([cosine, sine_part], axis=1)
    from_imag = jnp.stack([-sine_part, cosine], axis=1)
    return jnp.stack([from_real, from_imag], axis=1).reshape(2 * length, 2 * length)


def convolve(volume, weight, bias_vec):
    result = lax.conv_general_dilated(
        volume[None],
        weight,
        (1, 1, 1),
        [(0, 0), (1, 1), (1, 1)],
        dimension_numbers=("NCDHW", "OIDHW", "NCDHW"),
        preferred_element_type=jnp.float32,
    )[0]
    return jnp.maximum(result + bias_vec[:, None, None, None], 0.0)


def on_device(
    kspace,
    sensitivity,
    weight_first,
    bias_first,
    weight_second,
    bias_second,
    weight_third,
    bias_third,
):
    coil_count, rows_x, kz_local, twice_y = kspace.shape
    y_count = twice_y // 2
    kz_count = kz_local * lax.axis_size("kz")
    flat = kspace.reshape(-1, twice_y)
    y_lines = jnp.dot(
        flat, y_table(y_count), precision=HIGHEST_PRECISION, preferred_element_type=jnp.float32
    )
    y_lines = y_lines.reshape(coil_count, rows_x, kz_local, 2, y_count)
    z_matrix = z_stacked(kz_count)
    pieces = lax.all_to_all(y_lines, "kz", split_axis=4, concat_axis=2, tiled=True)
    coils_here, rows_here, kz_all, parts_here, y_here = pieces.shape
    grouped = pieces.reshape(coils_here * rows_here, kz_all * parts_here, y_here)
    product = lax.dot_general(
        grouped,
        z_matrix,
        (((1,), (0,)), ((), ())),
        precision=HIGHEST_PRECISION,
        preferred_element_type=jnp.float32,
    )
    coil_images = product.reshape(coils_here, rows_here, y_here, 2, kz_all)
    sens_view = jnp.transpose(sensitivity, (0, 2, 3, 1, 4))
    sens_re = sens_view[0]
    sens_im = sens_view[1]
    coil_re = coil_images[:, :, :, 0]
    coil_im = coil_images[:, :, :, 1]
    merged_re = jnp.sum(sens_re * coil_re + sens_im * coil_im, axis=0)
    merged_im = jnp.sum(sens_re * coil_im - sens_im * coil_re, axis=0)
    merged = jnp.stack([merged_re, merged_im], axis=0).astype(jnp.bfloat16)
    gathered = lax.all_to_all(merged, "kz", split_axis=3, concat_axis=2, tiled=True)
    slices = jnp.transpose(gathered, (0, 3, 1, 2))
    layers = ((weight_first, bias_first), (weight_second, bias_second), (weight_third, bias_third))
    activity = slices
    for weight, bias_vec in layers:
        extended = padded(activity, (("kz", 1),), 1)
        activity = convolve(extended, weight, bias_vec).astype(jnp.bfloat16)
    return activity


def solution(mesh):
    in_specs = (
        P("grp", None, "kz", None),
        P(None, ("grp", "kz"), None, None, None),
        P(),
        P(),
        P(),
        P(),
        P(),
        P(),
    )
    out_specs = P("grp", "kz", None, None)
    return jax.shard_map(
        on_device, mesh=mesh, in_specs=in_specs, out_specs=out_specs, check_vma=False
    )
```

profile of v0, /device:TPU:7, one launch (start us, length us, event | category | flops | bytes accessed | tf_op | source)
XLA Modules:
  0.0 860.8 jit_solution(986464142390691730)
XLA Ops:
  2.0 16.8 %convolution_bitcast_fusion = f32[2048,512]{0,1:T(8,128)} fusion(f32[2048,512]{1,0:T(8,128)} %bitcast.175, f32[256,256]{1,0:T(8,128)S(1)} %get-tuple-element.16, f32[256,256]{1,0:T(8,128)S(1)} %fusion.55, f32[256,256]{1,0:T(8,128)S(1)} %get-tuple-element.15), kind=kOutput, calls=%fused_computation.39 | convolution fusion | flops 6443237376 | bytes 9175040 | tf_op jit(solution)/shard_map/dot_general | solution.py:72
  18.8 5.4 copy.112
  24.2 5.9 reshape.101
  30.1 26.3 %copy.113 = f32[8,16,16,2,256]{2,1,3,0,4:T(8,128)} copy(f32[8,16,16,2,256]{4,3,2,1,0:T(2,128)} %reshape.101) | data formatting | bytes 8388608 | tf_op jit(solution)/shard_map/reshape | solution.py:75
  56.4 29.0 %reshape.144 = f32[32,1,32768]{2,1,0:T(1,128)} reshape(f32[256,8,2,16,16]{4,3,2,1,0:T(8,128)} %bitcast.163) | data formatting | bytes 8388608
  85.4 6.7 all-to-all-start
  92.1 3.9 fusion.48
  95.9 4.2 sine_multiply_fusion
  101.1 3.7 copy.117
  104.8 3.0 copy.148
  107.8 5.4 copy.118
  113.2 7.6 copy.150
  120.8 64.2 %all-to-all-done = f32[32,1,32768]{2,1,0:T(1,128)} async-done(((f32[32,1,32768]{2,1,0:T(1,128)}), f32[32,1,32768]{2,1,0:T(1,128)}, u32[]{:S(2)}, u32[]{:S(2)}) %all-to-all-start) | async-done | bytes 4194336 | tf_op jit(solution)/shard_map/all_to_all | solution.py:77
  185.5 14.5 %reduce = f32[32,32768]{1,0:T(8,128)} reduce(f32[32,1,32768]{2,1,0:T(1,128)} %all-to-all-done, f32[]{:T(128)} %broadcast.231), dimensions={1}, to_apply=%all_to_all.24.reduce_sub_computation | reduce | bytes 8388612 | tf_op jit(solution)/shard_map/all_to_all | solution.py:77
  200.0 28.9 %reshape.145 = f32[256,8,2,16,16]{4,3,2,1,0:T(8,128)} reshape(f32[32,32768]{1,0:T(8,128)} %reduce) | data formatting | bytes 8388608
  228.9 36.6 %copy.115 = f32[8,16,32,16,2,8]{1,0,5,4,3,2:T(8,128)} copy(f32[8,16,32,16,2,8]{3,1,4,0,5,2:T(8,128)} %bitcast.164) | data formatting | bytes 8388608 | tf_op jit(solution)/shard_map/all_to_all | solution.py:77
  265.5 21.4 %reshape.102 = f32[128,1024,8]{0,2,1:T(8,128)} reshape(f32[8,16,32,16,2,8]{1,0,5,4,3,2:T(8,128)} %copy.115) | data formatting | bytes 8388608 | tf_op jit(solution)/shard_map/reshape | solution.py:79
  286.9 5.6 copy.116
  292.5 16.8 %fusion.69 = f32[8,16,8,2,512]{4,2,3,1,0:T(8,128)S(1)} fusion(f32[8,16,8,1024,1]{3,2,4,1,0:T(8,128)} %bitcast.174, f32[2,512,1024,1,1]{2,1,0,4,3:T(8,128)} %bitcast.173), kind=kOutput, calls=%fused_computation.97 | convolution fusion | flops 12884901888 | bytes 12582912 | tf_op jit(solution)/shard_map/dot_general | solution.py:80
  314.8 13.3 %all_to_all.33 = bf16[32,2,2048]{2,1,0:T(2,128)(2,1)S(1)} all-to-all(bf16[32,2,2048]{2,1,0:T(2,128)(2,1)S(1)} %reshape.146), channel_id=1, replica_groups=mesh['grp'=1,'kz'=32] {'kz'}, dimensions={0} | all-to-all | bytes 524288 | tf_op jit(solution)/shard_map/all_to_all | solution.py:96
  330.4 4.0 copy.122
  334.4 2.9 fusion.68
  339.3 4.4 collective-permute-start
  348.5 4.0 collective-permute-done.1
  353.7 9.0 %copy.127 = bf16[2,18,16,1,8,33]{4,0,5,2,1,3:T(2,128)(2,1)} copy(bf16[2,18,16,1,8,33]{5,4,2,1,0,3:T(8,128)(2,1)S(1)} %reshape.106) | data formatting | bytes 608256 | tf_op jit(solution)/shard_map/conv_general_dilated | solution.py:47
  364.1 15.1 %fusion.82 = bf16[2,18,16,8,35]{3,0,4,2,1:T(2,128)(2,1)S(1)} fusion(bf16[2,18,16,1,7,2]{4,0,5,2,1,3:T(2,128)(2,1)S(1)} %slice.52, bf16[2,18,16,1,8,33]{4,0,5,2,1,3:T(2,128)(2,1)} %copy.127), kind=kLoop, calls=%fused_computation.34.clone.clone.1 | loop fusion | flops 967680 | bytes 642816 | tf_op jit(solution)/shard_map/conv_general_dilated | solution.py:47
  379.3 55.2 %convolution_select_fusion = f32[16,16,8,33,24]{4,2,3,1,0:T(8,128)} fusion(bf16[24,2,3,3,3]{0,1,4,3,2:T(2,128)(2,1)S(1)} %copy-done.7, pred[8,33]{0,1:T(8,128)(4,1)S(1)} %copy-done.8, bf16[2,18,16,8,35]{3,0,4,2,1:T(2,128)(2,1)S(1)} %fusion.82), kind=kOutput, calls=%fused_computation.16 | convolution fusion | flops 169500672 | bytes 6813480 | tf_op jit(solution)/shard_map/conv_general_dilated | solution.py:47
  434.5 32.2 %copy.128 = f32[16,16,8,33,24]{3,2,4,1,0:T(8,128)} copy(f32[16,16,8,33,24]{4,2,3,1,0:T(8,128)} %convolution_select_fusion) | data formatting | bytes 12976128 | tf_op jit(solution)/shard_map/conv_general_dilated | solution.py:47
  466.7 20.1 %reshape.110 = f32[16,16,1,264,24]{3,4,1,0,2:T(8,128)} reshape(f32[16,16,8,33,24]{3,2,4,1,0:T(8,128)} %copy.128) | data formatting | bytes 12976128 | tf_op jit(solution)/shard_map/conv_general_dilated | solution.py:47
  486.8 3.6 fusion.30
  492.4 2.4 collective-permute-start.3
  495.0 6.2 collective-permute-done.3
  501.7 4.9 pad.2
  506.5 19.1 %reshape.142 = bf16[24,18,16,1,8,33]{5,4,0,2,1,3:T(8,128)(2,1)} reshape(bf16[24,18,16,1,264]{4,0,2,1,3:T(8,128)(2,1)} %pad.2) | data formatting | bytes 7299072 | tf_op jit(solution)/shard_map/conv_general_dilated | solution.py:47
  525.6 27.5 %copy.131 = bf16[24,18,16,1,8,33]{0,4,5,2,1,3:T(8,128)(2,1)} copy(bf16[24,18,16,1,8,33]{5,4,0,2,1,3:T(8,128)(2,1)} %reshape.142) | data formatting | bytes 7299072 | tf_op jit(solution)/shard_map/conv_general_dilated | solution.py:47
  554.8 63.6 %broadcast_select_fusion.1 = f32[16,16,8,33,24]{4,2,3,1,0:T(8,128)} fusion(pred[8,33]{0,1:T(8,128)(4,1)S(1)} %copy-done.8, bf16[24,24,3,3,3]{1,0,4,3,2:T(8,128)(2,1)S(1)} %copy-done, bf16[24,18,16,1,7,2]{0,4,5,2,1,3:T(8,128)(2,1)S(1)} %slice.56, bf16[24,18,16,1,8,33]{0,4,5,2,1,3:T(8,128)(2,1)} %copy.131), kind=kOutput, calls=%fused_computation.18 | convolution fusion | flops 2027778048 | bytes 10362504 | tf_op jit(solution)/shard_map/conv_general_dilated | solution.py:47
  618.3 32.0 %copy.132 = f32[16,16,8,33,24]{3,2,4,1,0:T(8,128)} copy(f32[16,16,8,33,24]{4,2,3,1,0:T(8,128)} %broadcast_select_fusion.1) | data formatting | bytes 12976128 | tf_op jit(solution)/shard_map/conv_general_dilated | solution.py:47
  650.4 20.1 %reshape.117 = f32[16,16,1,264,24]{3,4,1,0,2:T(8,128)} reshape(f32[16,16,8,33,24]{3,2,4,1,0:T(8,128)} %copy.132) | data formatting | bytes 12976128 | tf_op jit(solution)/shard_map/conv_general_dilated | solution.py:47
  670.5 3.6 fusion.27
  676.1 2.4 collective-permute-start.5
  678.7 6.2 collective-permute-done.5
  685.6 4.9 pad.4
  690.4 19.1 %reshape.143 = bf16[24,18,16,1,8,33]{5,4,0,2,1,3:T(8,128)(2,1)} reshape(bf16[24,18,16,1,264]{4,0,2,1,3:T(8,128)(2,1)} %pad.4) | data formatting | bytes 7299072 | tf_op jit(solution)/shard_map/conv_general_dilated | solution.py:47
  709.5 27.5 %copy.135 = bf16[24,18,16,1,8,33]{0,4,5,2,1,3:T(8,128)(2,1)} copy(bf16[24,18,16,1,8,33]{5,4,0,2,1,3:T(8,128)(2,1)} %reshape.143) | data formatting | bytes 7299072 | tf_op jit(solution)/shard_map/conv_general_dilated | solution.py:47
  738.7 63.5 %broadcast_select_fusion = f32[16,16,8,33,24]{4,2,3,1,0:T(8,128)} fusion(pred[8,33]{0,1:T(8,128)(4,1)S(1)} %copy-done.8, bf16[24,24,3,3,3]{1,0,4,3,2:T(8,128)(2,1)S(1)} %copy-done.6, bf16[24,18,16,1,7,2]{0,4,5,2,1,3:T(8,128)(2,1)S(1)} %slice.60, bf16[24,18,16,1,8,33]{0,4,5,2,1,3:T(8,128)(2,1)} %copy.135), kind=kOutput, calls=%fused_computation.17 | convolution fusion | flops 2027778048 | bytes 10362504 | tf_op jit(solution)/shard_map/conv_general_dilated | solution.py:47
  802.2 32.0 %copy.136 = f32[16,16,8,33,24]{3,2,4,1,0:T(8,128)} copy(f32[16,16,8,33,24]{4,2,3,1,0:T(8,128)} %broadcast_select_fusion) | data formatting | bytes 12976128 | tf_op jit(solution)/shard_map/conv_general_dilated | solution.py:47
  834.3 20.1 %reshape.124 = f32[16,16,1,264,24]{3,4,1,0,2:T(8,128)} reshape(f32[16,16,8,33,24]{3,2,4,1,0:T(8,128)} %copy.136) | data formatting | bytes 12976128 | tf_op jit(solution)/shard_map/conv_general_dilated | solution.py:47
  854.4 3.6 fusion.24
  (48 shorter events, 31.9 us)
Async XLA Ops:
  0.0 554.8 %copy-start = (bf16[24,24,3,3,3]{1,0,4,3,2:T(8,128)(2,1)S(1)}, bf16[24,24,3,3,3]{1,0,4,3,2:T(8,128)(2,1)}, u32[]{:S(2)}) copy-start(bf16[24,24,3,3,3]{1,0,4,3,2:T(8,128)(2,1)} %param.12) | copy-start | bytes 93316
  85.4 99.6 %all-to-all-start = ((f32[32,1,32768]{2,1,0:T(1,128)}), f32[32,1,32768]{2,1,0:T(1,128)}, u32[]{:S(2)}, u32[]{:S(2)}) async-start(f32[32,1,32768]{2,1,0:T(1,128)} %reshape.144), calls=%async_computation | async-start | bytes 8388608 | tf_op jit(solution)/shard_map/all_to_all | solution.py:77
  292.5 16.8 %copy-start.2 = (f32[2,8,8,16,512]{4,1,3,2,0:T(8,128)S(1)}, f32[2,8,8,16,512]{4,1,3,2,0:T(8,128)}, u32[]{:S(2)}) copy-start(f32[2,8,8,16,512]{4,1,3,2,0:T(8,128)} %copy.150) | copy-start | bytes 12582916
  339.3 9.2 %collective-permute-start = (bf16[2,1,16,256]{3,2,1,0:T(8,128)(2,1)S(1)}, bf16[2,1,16,256]{3,2,1,0:T(8,128)(2,1)S(1)}, u32[]{:S(2)}, u32[]{:S(2)}) collective-permute-start(bf16[2,1,16,256]{3,2,1,0:T(8,128)(2,1)S(1)} %copy.123), channel_id=1, source_target_pairs={{0,1},{1,2},{2,3},{3,4},{4,5},{5,6},{6,7},{7,8},{8,9},{9,10},{10,1... | collective-permute-start | bytes 49160 | tf_op jit(solution)/shard_map/ppermute | solution.py:18
  345.6 6.9 collective-permute-start.1
  364.1 15.1 %copy-start.7 = (bf16[24,2,3,3,3]{0,1,4,3,2:T(2,128)(2,1)S(1)}, bf16[24,2,3,3,3]{0,1,4,3,2:T(2,128)(2,1)}, u32[]{:S(2)}) copy-start(bf16[24,2,3,3,3]{0,1,4,3,2:T(2,128)(2,1)} %param.10) | copy-start | bytes 7780
  364.1 15.1 %copy-start.8 = (pred[8,33]{0,1:T(8,128)(4,1)S(1)}, pred[8,33]{0,1:T(8,128)(4,1)}, u32[]{:S(2)}) copy-start(pred[8,33]{0,1:T(8,128)(4,1)} %constant.54) | copy-start | bytes 796
  466.7 20.1 %copy-start.3 = (f32[24]{0:T(128)S(1)}, f32[24]{0:T(128)}, u32[]{:S(2)}) copy-start(f32[24]{0:T(128)} %param.11) | copy-start | bytes 292
  490.5 4.5 collective-permute-start.2
  492.4 8.8 %collective-permute-start.3 = (bf16[24,1,16,256]{3,0,2,1:T(8,128)(2,1)S(1)}, bf16[24,1,16,256]{3,0,2,1:T(8,128)(2,1)S(1)}, u32[]{:S(2)}, u32[]{:S(2)}) collective-permute-start(bf16[24,1,16,256]{3,0,2,1:T(8,128)(2,1)S(1)} %get-tuple-element.10), channel_id=1, source_target_pairs={{1,0},{2,1},{3,2},{4,3},{5,4},{6,5},{7,6},{8,7},{9,8},{10,9},{11,1... | collective-permute-start | bytes 589832 | tf_op jit(solution)/shard_map/ppermute | solution.py:19
  650.4 20.1 %copy-start.4 = (f32[24]{0:T(128)S(1)}, f32[24]{0:T(128)}, u32[]{:S(2)}) copy-start(f32[24]{0:T(128)} %param.13) | copy-start | bytes 292
  674.1 4.5 collective-permute-start.4
  676.1 8.8 %collective-permute-start.5 = (bf16[24,1,16,256]{3,0,2,1:T(8,128)(2,1)S(1)}, bf16[24,1,16,256]{3,0,2,1:T(8,128)(2,1)S(1)}, u32[]{:S(2)}, u32[]{:S(2)}) collective-permute-start(bf16[24,1,16,256]{3,0,2,1:T(8,128)(2,1)S(1)} %get-tuple-element.8), channel_id=1, source_target_pairs={{1,0},{2,1},{3,2},{4,3},{5,4},{6,5},{7,6},{8,7},{9,8},{10,9},{11,1... | collective-permute-start | bytes 589832 | tf_op jit(solution)/shard_map/ppermute | solution.py:19
  709.5 29.2 %copy-start.6 = (bf16[24,24,3,3,3]{1,0,4,3,2:T(8,128)(2,1)S(1)}, bf16[24,24,3,3,3]{1,0,4,3,2:T(8,128)(2,1)}, u32[]{:S(2)}) copy-start(bf16[24,24,3,3,3]{1,0,4,3,2:T(8,128)(2,1)} %param.14) | copy-start | bytes 93316
  834.3 20.1 %copy-start.5 = (f32[24]{0:T(128)S(1)}, f32[24]{0:T(128)}, u32[]{:S(2)}) copy-start(f32[24]{0:T(128)} %param.15) | copy-start | bytes 292
  854.4 6.0 copy-start.1
where the time goes:
time: 877 us; the launch traced here: 861 us
  local copies, waits for them, and re-layouts  475 us (54%)
  matrix products  216 us (25%)
  waiting for transfers between devices  81 us (9%)
  other arithmetic  53.8 us (6%)
  starting transfers between devices  21.6 us (2%)
  blocking collectives  13.3 us (2%)
    conv_general_dilated x15, local copies, waits for them, and re-layouts, convolve(): lax.conv_general_dilated(volume[None], weight, (1, 1, 1), [(0, 0), (1, 1)...  265 us
    conv_general_dilated x3, matrix products, convolve(): lax.conv_general_dilated(volume[None], weight, (1, 1, 1), [(0, 0), (1, 1)...  182 us
    unnamed x24, local copies, waits for them, and re-layouts  73.1 us
    all_to_all x1, waiting for transfers between devices, on_device(): lax.all_to_all(y_lines, 'kz', split_axis=4, concat_axis=2, tiled=True)  64.2 us
    all_to_all x2, local copies, waits for them, and re-layouts, on_device(): lax.all_to_all(y_lines, 'kz', split_axis=4, concat_axis=2, tiled=True)  37.1 us
    reshape x2, local copies, waits for them, and re-layouts, on_device(): y_lines = y_lines.reshape(coil_count, rows_x, kz_local, 2, y_count)  32.2 us
    reshape x1, local copies, waits for them, and re-layouts, on_device(): pieces.reshape(coils_here * rows_here, kz_all * parts_here, y_here)  21.4 us
  transfers between devices with their start and end apart: 7, of which 6 were waited for; matrix products, arithmetic and copies ran while one was open for 4% of the time, Pallas kernels for 0%

commit v1 on v0

v1 whole, which is shorter than its diff:
```python
import functools
import math

import jax
import jax.numpy as jnp
import numpy as np
from jax import lax
from jax.experimental import pallas as pl
from jax.experimental.pallas import tpu as pltpu
from jax.sharding import PartitionSpec as P

BF16 = jnp.bfloat16
F32 = jnp.float32
HALO = 3
WINDOW = 256
VMEM_LIMIT = 56 * 1024 * 1024


def round_up(value, unit):
    return -(-value // unit) * unit


def params():
    return pltpu.CompilerParams(vmem_limit_bytes=VMEM_LIMIT)


def vmem_spec():
    return pl.BlockSpec(memory_space=pltpu.VMEM)


def halves(table):
    high = table.astype(jnp.bfloat16)
    low = (table - high.astype(np.float64)).astype(jnp.bfloat16)
    return high, low


def trig(length, rows, cols):
    phase = (rows[:, None] * cols[None, :]) % length
    angle = phase * (2.0 * math.pi / length)
    return np.cos(angle), np.sin(angle)


def y_table(y_count, devices):
    y_here = y_count // devices
    order = (np.arange(devices)[None, :] * y_here + np.arange(y_here)[:, None]).reshape(-1)
    cosine, sine = trig(y_count, order, np.arange(y_count))
    real = np.concatenate([cosine, -sine], axis=1)
    imag = np.concatenate([sine, cosine], axis=1)
    table = np.stack([real, imag], axis=1).reshape(2 * y_count, 2 * y_count)
    return table / math.sqrt(y_count)


def z_table(z_count, devices):
    cosine, sine = trig(z_count, np.arange(z_count), np.arange(z_count))
    real = np.concatenate([cosine, sine], axis=1)
    imag = np.concatenate([-sine, cosine], axis=1)
    table = np.stack([real, imag], axis=0).reshape(2, devices, z_count // devices, 2 * z_count)
    return np.transpose(table, (1, 0, 2, 3)).reshape(2 * z_count, 2 * z_count)


def y_kernel(devices, k_ref, t_ref, out_ref, lines, turned, sems):
    pairs, kz_here, width = lines.shape[1], lines.shape[0], lines.shape[2]
    rows = t_ref.shape[0]

    def fetch(kz):
        return pltpu.make_async_copy(k_ref.at[:, kz, :], lines.at[kz], sems.at[kz])

    for kz in range(kz_here):
        fetch(kz).start()
    for kz in range(kz_here):
        fetch(kz).wait()
        line = lines[kz]
        high = line.astype(BF16)
        low = (line - high.astype(F32)).astype(BF16)
        operand = jnp.concatenate([high, high, low], axis=1)
        result = lax.dot_general(
            t_ref[...], operand, (((1,), (1,)), ((), ())), preferred_element_type=F32
        )
        turned[pl.ds(kz, rows, stride=kz_here), :] = result
    block = 2 * kz_here
    for row in range(rows // 2):
        y, device = row // devices, row % devices
        out_ref[device, :, y * pairs : (y + 1) * pairs] = turned[
            row * block : (row + 1) * block, :
        ].astype(BF16)


def y_transform(kspace, devices):
    coils, xs, kz_here, width = kspace.shape
    pairs = coils * xs
    y_count = width // 2
    high, low = halves(y_table(y_count, devices))
    table = jnp.asarray(np.concatenate([high, low, high], axis=1))
    return pl.pallas_call(
        functools.partial(y_kernel, devices),
        out_shape=jax.ShapeDtypeStruct((devices, 2 * kz_here, y_count // devices * pairs), BF16),
        in_specs=[pl.BlockSpec(memory_space=pl.ANY), vmem_spec()],
        out_specs=vmem_spec(),
        scratch_shapes=[
            pltpu.VMEM((kz_here, pairs, width), F32),
            pltpu.VMEM((2 * y_count * kz_here, pairs), F32),
            pltpu.SemaphoreType.DMA((kz_here,)),
        ],
        compiler_params=params(),
    )(kspace.reshape(pairs, kz_here, width), table)


def z_kernel(scale, devices, y_here, r_ref, t_ref, s_ref, out_ref, merged, turned):
    step = pl.program_id(0)
    coils, xs, z_count = s_ref.shape[2:]
    z_here = z_count // devices
    lines = r_ref[...].T
    operand = jnp.concatenate([lines, lines], axis=1)
    images = jnp.dot(operand, t_ref[...], preferred_element_type=F32)
    image_re = images[:, :z_count].reshape(coils, xs, z_count)
    image_im = images[:, z_count:].reshape(coils, xs, z_count)
    sens_re = s_ref[0, 0]
    sens_im = s_ref[1, 0]
    real = jnp.sum(sens_re * image_re + sens_im * image_im, axis=0) * scale
    imag = jnp.sum(sens_re * image_im - sens_im * image_re, axis=0) * scale
    base = pl.multiple_of(step * 2 * xs, 2 * xs)

    if merged.shape[0] > y_here * 2 * xs:

        @pl.when(step == 0)
        def _():
            merged[...] = jnp.zeros_like(merged)

    merged[pl.ds(base, 2 * xs), :] = jnp.concatenate([real, imag], axis=0)

    @pl.when(step == pl.num_programs(0) - 1)
    def _():
        lanes = merged.shape[0]
        rows = out_ref.shape[1]
        turned[...] = jnp.zeros_like(turned)
        turned[8 : 8 + z_count, :] = merged[...].T
        for device in range(devices):
            first = 8 + device * z_here - HALO
            out_ref[device] = turned[first : first + rows, :].astype(BF16)


def z_transform(received, sensitivity, devices):
    _, y_here, coils, xs, z_count = sensitivity.shape
    pairs = coils * xs
    high, low = halves(z_table(z_count, devices))
    table = jnp.asarray(np.concatenate([high, low], axis=0))
    scale = 1.0 / math.sqrt(z_count)
    rows = round_up(z_count // devices + 2 * HALO, 8)
    lanes = round_up(y_here * 2 * xs, 128)
    flat = received.reshape(2 * z_count, y_here * pairs)
    return pl.pallas_call(
        functools.partial(z_kernel, scale, devices, y_here),
        out_shape=jax.ShapeDtypeStruct((devices, rows, lanes), BF16),
        grid=(y_here,),
        in_specs=[
            pl.BlockSpec((2 * z_count, pairs), lambda y: (0, y)),
            pl.BlockSpec(table.shape, lambda y: (0, 0)),
            pl.BlockSpec((2, 1, coils, xs, z_count), lambda y: (0, y, 0, 0, 0)),
        ],
        out_specs=pl.BlockSpec((devices, rows, lanes), lambda y: (0, 0, 0)),
        scratch_shapes=[
            pltpu.VMEM((lanes, z_count), F32),
            pltpu.VMEM((8 + z_count + 32, lanes), F32),
        ],
        compiler_params=params(),
    )(flat, table, sensitivity)


def window_starts(lanes):
    return (0, lanes - WINDOW)


def column_map(xs, channels, x_major):
    half = xs // 2
    found = []
    for h in range(2):
        x, c = np.meshgrid(np.arange(half) + h * half, np.arange(channels), indexing="ij")
        if x_major:
            pad = np.full(WINDOW - half * channels, -9)
            x, c = x.reshape(-1), c.reshape(-1)
            order = [(pad, x), (pad, c)] if h else [(x, pad), (c, pad)]
            found.append((np.concatenate(order[0]), np.concatenate(order[1])))
        else:
            found.append((x.T.reshape(-1), c.T.reshape(-1)))
    return found


def band_masks(x_in, x_out):
    taps = np.arange(3)[:, None, None]
    return (x_in[None, :, None] == x_out[None, None, :] + taps - 1).astype(np.float32)


def spread_maps(xs, channels, x_major):
    rows_of, columns_of, masks = [], [], []
    lanes = xs * channels
    for start, (x_out, c_out) in zip(window_starts(lanes), column_map(xs, channels, x_major)):
        lane = start + np.arange(WINDOW)
        rows_of.append(lane[:, None] % channels == np.arange(channels)[None, :])
        columns_of.append(np.arange(channels)[:, None] == c_out[None, :])
        masks.append(band_masks(lane // channels, x_out))
    return [jnp.asarray(np.stack(m).astype(np.float32), BF16) for m in (rows_of, columns_of, masks)]


def first_maps(parts, xs, channels):
    row = np.arange(parts * xs)
    lane = np.arange(xs * channels)
    rows_of = row[:, None] // xs == np.arange(parts)[None, :]
    columns_of = np.arange(channels)[:, None] == lane[None, :] % channels
    masks = band_masks(row % xs, lane // channels)
    return [jnp.asarray(np.asarray(m, np.float32), BF16) for m in (rows_of, columns_of, masks)]


def spread_tap(kernel_ref, tap, rows_of, columns_of, masks):
    total = None
    for dx in range(3):
        tall = jnp.dot(rows_of, kernel_ref[tap, dx], preferred_element_type=F32).astype(BF16)
        wide = jnp.dot(tall, columns_of, preferred_element_type=F32)
        term = wide * masks[dx].astype(F32)
        total = term if total is None else total + term
    return total.astype(BF16)


def expand_kernel(
    y_here,
    k1_ref,
    k2_ref,
    k3_ref,
    r1_ref,
    c1_ref,
    m1_ref,
    r2_ref,
    c2_ref,
    m2_ref,
    r3_ref,
    c3_ref,
    m3_ref,
    w1_ref,
    side_ref,
    w2_ref,
    w3_ref,
):
    piece = r1_ref.shape[0]
    full = w1_ref.shape[1] // 3
    w1_ref[...] = jnp.zeros_like(w1_ref)
    side_ref[...] = jnp.zeros_like(side_ref)
    for dz in range(3):
        for dy in range(3):
            tap = dz * 3 + dy
            block = spread_tap(k1_ref, tap, r1_ref[...], c1_ref[...], m1_ref)
            for m in range(y_here):
                y = m + dy - 1
                if 0 <= y < y_here:
                    base = dz * full + y * piece
                    w1_ref[m, base : base + piece, :] = block
            if dy == 0:
                base = dz * full + (y_here - 1) * piece
                side_ref[0, base : base + piece, :] = block
            if dy == 2:
                side_ref[1, dz * full : dz * full + piece, :] = block

    def deep(tap, carry):
        base = pl.multiple_of(tap * WINDOW, WINDOW)
        for h in range(2):
            w2_ref[h, pl.ds(base, WINDOW), :] = spread_tap(
                k2_ref, tap, r2_ref[h], c2_ref[h], m2_ref.at[h]
            )
            w3_ref[h, pl.ds(base, WINDOW), :] = spread_tap(
                k3_ref, tap, r3_ref[h], c3_ref[h], m3_ref.at[h]
            )
        return carry

    lax.fori_loop(0, 9, deep, 0)


def expand_weights(first, second, third, y_here, xs):
    channels, parts = first.shape[:2]
    full = round_up(y_here * parts * xs, 128)
    lanes = xs * channels
    by_tap = [
        jnp.transpose(w, (2, 4, 3, 1, 0)).reshape(9, 3, w.shape[1], channels)
        for w in (first, second, third)
    ]
    maps = first_maps(parts, xs, channels)
    maps += spread_maps(xs, channels, True) + spread_maps(xs, channels, False)
    return pl.pallas_call(
        functools.partial(expand_kernel, y_here),
        out_shape=(
            jax.ShapeDtypeStruct((y_here, 3 * full, lanes), BF16),
            jax.ShapeDtypeStruct((2, 3 * full, lanes), BF16),
            jax.ShapeDtypeStruct((2, 9 * WINDOW, WINDOW), BF16),
            jax.ShapeDtypeStruct((2, 9 * WINDOW, xs // 2 * channels), BF16),
        ),
        in_specs=[vmem_spec()] * 12,
        out_specs=(vmem_spec(),) * 4,
        compiler_params=params(),
        cost_estimate=pl.CostEstimate(
            flops=20_000_000_000, bytes_accessed=10_000_000, transcendentals=0
        ),
    )(*by_tap, *maps)


def join(left, right):
    return jnp.concatenate(
        [left[:, :128], left[:, 128:] + right[:, :128], right[:, 128:]], axis=1
    )


def down_one(block):
    rolled = pltpu.roll(block, 1, 0)
    row = lax.broadcasted_iota(jnp.int32, block.shape, 0)
    return jnp.where(row == 0, 0.0, rolled)


def up_one(block):
    count = block.shape[0]
    rolled = pltpu.roll(block, count - 1, 0)
    row = lax.broadcasted_iota(jnp.int32, block.shape, 0)
    return jnp.where(row == count - 1, 0.0, rolled)


def net_kernel(
    place_ref,
    in_ref,
    w1_ref,
    w1_side_ref,
    w2_ref,
    w3_ref,
    b12_ref,
    b3_ref,
    order_ref,
    out_ref,
    spread,
    own,
    before,
    after,
    act1,
    act2,
):
    devices, rows_in, lanes_in = in_ref.shape
    z1, groups = act1.shape[:2]
    z2 = act2.shape[0]
    z_here = z2 - 2
    y_here = groups - 2
    first_z = place_ref[0]
    z_count = place_ref[1]
    window = 256
    lanes = act1.shape[3]

    def taps(act, z, h):
        start = h * (lanes - window)
        pieces = []
        for dz in range(3):
            for dy in range(3):
                piece = act[z + dz, dy : dy + y_here, :, start : start + window]
                pieces.append(piece.reshape(y_here * devices, window))
        return jnp.concatenate(pieces, axis=1)

    def inside(z):
        return jnp.where((z >= 0) & (z < z_count), 1.0, 0.0).astype(F32)

    @pl.when(pl.program_id(0) == 0)
    def _():
        for s in range(devices):
            piece = in_ref[s].astype(F32)
            for j in range(0, lanes_in, 128):
                spread[j // 128, pl.ds(s, rows_in, stride=devices), :] = piece[:, j : j + 128]

        tiles = [spread.at[j] for j in range(lanes_in // 128)]

        def shift(z, carry):
            base = pl.multiple_of(z * devices, devices)
            block = jnp.concatenate([part[pl.ds(base, devices), :] for part in tiles], axis=1)
            own[pl.ds(base, devices), :] = block.astype(BF16)
            before[pl.ds(base, devices), :] = down_one(block).astype(BF16)
            after[pl.ds(base, devices), :] = up_one(block).astype(BF16)
            return carry

        lax.fori_loop(0, z1 + 2, shift, 0)

        def first(z, carry):
            def three(ref):
                pieces = []
                for dz in range(3):
                    base = pl.multiple_of((z + dz) * devices, devices)
                    pieces.append(ref[pl.ds(base, devices), :])
                return jnp.concatenate(pieces, axis=1)

            mask = inside(first_z + z - 2)
            middle = three(own)
            for m in range(y_here):
                result = jnp.dot(middle, w1_ref[m], preferred_element_type=F32)
                if m == 0:
                    result += jnp.dot(three(before), w1_side_ref[0], preferred_element_type=F32)
                if m == y_here - 1:
                    result += jnp.dot(three(after), w1_side_ref[1], preferred_element_type=F32)
                value = jnp.maximum(result + b12_ref[0:1, :], 0.0) * mask
                act1[z, m + 1] = value.astype(BF16)
                if m == 0:
                    act1[z, groups - 1] = up_one(value).astype(BF16)
                if m == y_here - 1:
                    act1[z, 0] = down_one(value).astype(BF16)
            return carry

        lax.fori_loop(0, z1, first, 0)

        def second(z, carry):
            left = jnp.dot(taps(act1, z, 0), w2_ref[0], preferred_element_type=F32)
            right = jnp.dot(taps(act1, z, 1), w2_ref[1], preferred_element_type=F32)
            mask = inside(first_z + z - 1)
            value = jnp.maximum(join(left, right) + b12_ref[1:2, :], 0.0) * mask
            cube = value.reshape(y_here, devices, lanes)
            act2[z, 1 : groups - 1] = cube.astype(BF16)
            act2[z, groups - 1] = up_one(cube[0]).astype(BF16)
            act2[z, 0] = down_one(cube[y_here - 1]).astype(BF16)
            return carry

        lax.fori_loop(0, z2, second, 0)

    z = pl.program_id(0)
    channels, _, xs, y_count = out_ref.shape
    parts = []
    for h in range(2):
        result = jnp.dot(taps(act2, z, h), w3_ref[h], preferred_element_type=F32)
        value = jnp.maximum(result + b3_ref[...], 0.0).astype(BF16)
        turned = lax.dot_general(
            value, order_ref[...], (((0,), (0,)), ((), ())), preferred_element_type=F32
        )
        parts.append(turned.reshape(channels, xs // 2, y_count))
    out_ref[:, 0] = jnp.concatenate(parts, axis=1).astype(BF16)


def network(gathered, place, weights, biases, z_here, xs, y_here):
    devices, rows_in, lanes_in = gathered.shape
    channels = biases[0].shape[0]
    y_count = y_here * devices
    lanes = xs * channels
    w1, w1_side, w2, w3 = weights
    b12 = jnp.stack([jnp.tile(biases[0], xs), jnp.tile(biases[1], xs)])
    b3 = jnp.repeat(biases[2], xs // 2)[None]
    row = np.arange(y_count)
    order = np.zeros((y_count, y_count), np.float32)
    order[row, row % devices * y_here + row // devices] = 1.0
    order = jnp.asarray(order, BF16)
    z1, z2 = z_here + 4, z_here + 2
    groups = y_here + 2
    return pl.pallas_call(
        net_kernel,
        out_shape=jax.ShapeDtypeStruct((channels, z_here, xs, y_count), BF16),
        grid=(z_here,),
        in_specs=[pl.BlockSpec(memory_space=pltpu.SMEM)] + [vmem_spec()] * 8,
        out_specs=pl.BlockSpec((channels, 1, xs, y_count), lambda z: (0, z, 0, 0)),
        scratch_shapes=[
            pltpu.VMEM((lanes_in // 128, rows_in * devices, 128), F32),
            pltpu.VMEM((rows_in * devices, lanes_in), BF16),
            pltpu.VMEM((rows_in * devices, lanes_in), BF16),
            pltpu.VMEM((rows_in * devices, lanes_in), BF16),
            pltpu.VMEM((z1, groups, devices, lanes), BF16),
            pltpu.VMEM((z2, groups, devices, lanes), BF16),
        ],
        compiler_params=params(),
    )(place, gathered, w1, w1_side, w2, w3, b12, b3, order)


def on_device(
    kspace,
    sensitivity,
    weight_first,
    bias_first,
    weight_second,
    bias_second,
    weight_third,
    bias_third,
):
    devices = lax.axis_size("kz")
    _, y_here, _, xs, z_count = sensitivity.shape
    z_here = z_count // devices
    lines = y_transform(kspace, devices)
    received = lax.all_to_all(lines, "kz", 0, 0)
    weights = expand_weights(weight_first, weight_second, weight_third, y_here, xs)
    received, weights = lax.optimization_barrier((received, weights))
    merged = z_transform(received, sensitivity, devices)
    gathered = lax.all_to_all(merged, "kz", 0, 0)
    place = jnp.stack([lax.axis_index("kz") * z_here, z_count]).astype(jnp.int32)
    biases = (bias_first, bias_second, bias_third)
    return network(gathered, place, weights, biases, z_here, xs, y_here)


def solution(mesh):
    in_specs = (
        P("grp", None, "kz", None),
        P(None, ("grp", "kz"), None, None, None),
        P(),
        P(),
        P(),
        P(),
        P(),
        P(),
    )
    out_specs = P("grp", "kz", None, None)
    return jax.shard_map(
        on_device, mesh=mesh, in_specs=in_specs, out_specs=out_specs, check_vma=False
    )
```

time: 877 us -> 177 us (0.20)
  the two profiles are of different devices: /device:TPU:7 before, /device:TPU:0 now
where the time goes in v1:
time: 177 us; the launch traced here: 176 us
  Pallas kernels  121 us (68%)
  waiting for transfers between devices  37.5 us (21%)
  starting transfers between devices  11.5 us (6%)
  local copies, waits for them, and re-layouts  5.24 us (3%)
    pallas_call x1, Pallas kernels, network(): pl.pallas_call(net_kernel, out_shape=jax.ShapeDtypeStruct((channels, z_he...  69.7 us
    all_to_all x1, waiting for transfers between devices, on_device(): received = lax.all_to_all(lines, 'kz', 0, 0)  26.7 us
    pallas_call x1, Pallas kernels, y_transform(): pl.pallas_call(functools.partial(y_kernel, devices), out_shape=jax.ShapeD...  20 us
    pallas_call x1, Pallas kernels, expand_weights(): pl.pallas_call(functools.partial(expand_kernel, y_here), out_shape=(jax.S...  19.9 us
    pallas_call x1, Pallas kernels, z_transform(): pl.pallas_call(functools.partial(z_kernel, scale, devices, y_here), out_s...  11 us
    all_to_all x1, waiting for transfers between devices, on_device(): gathered = lax.all_to_all(merged, 'kz', 0, 0)  10.8 us
    all_to_all x1, starting transfers between devices, on_device(): received = lax.all_to_all(lines, 'kz', 0, 0)  7.3 us
    all_to_all x1, starting transfers between devices, on_device(): gathered = lax.all_to_all(merged, 'kz', 0, 0)  4.2 us
  transfers between devices with their start and end apart: 2, of which 2 were waited for; matrix products, arithmetic and copies ran while one was open for 2% of the time, Pallas kernels for 11%

profile of v1, /device:TPU:0, one launch (start us, length us, event | category | flops | bytes accessed | tf_op | source)
XLA Modules:
  0.0 176.2 jit_solution(5456617162330985037)
XLA Ops:
  0.0 20.0 %shard_map.190 = bf16[32,32,1024]{2,1,0:T(8,128)(2,1)} custom-call(f32[128,16,512]{2,1,0:T(8,128)} %bitcast.10, bf16[512,1536]{1,0:T(8,128)(2,1)} %constant.30.clone.t_ref), custom_call_target="tpu_custom_call" | custom-call | tf_op jit(solution)/shard_map/pallas_call | solution.py:94
  20.0 0.0 copy-start.4
  20.0 0.0 copy-start.2
  20.0 0.0 copy-start.3
  20.0 7.3 %all-to-all-start = ((bf16[32,32,1024]{2,1,0:T(8,128)(2,1)}), bf16[32,32,1024]{2,1,0:T(8,128)(2,1)S(1)}, u32[]{:S(2)}, u32[]{:S(2)}) async-start(bf16[32,32,1024]{2,1,0:T(8,128)(2,1)} %shard_map.190), calls=%async_computation | async-start | bytes 4194304 | tf_op jit(solution)/shard_map/all_to_all | solution.py:478
  27.3 0.0 copy-done.4
  27.3 0.6 copy.24
  27.9 0.0 copy-done.2
  28.0 0.8 copy.25
  28.8 0.0 copy-done.3
  28.8 0.8 copy.26
  29.6 19.9 %shard_map.191 = (bf16[8,768,384]{2,1,0:T(8,128)(2,1)}, bf16[2,768,384]{2,1,0:T(8,128)(2,1)}, bf16[2,2304,256]{2,1,0:T(8,128)(2,1)}, bf16[2,2304,192]{2,1,0:T(8,128)(2,1)}) custom-call(bf16[9,3,2,24]{3,2,1,0:T(2,128)(2,1)} %bitcast.16, bf16[9,3,24,24]{3,2,1,0:T(8,128)(2,1)} %bitcast.13, bf16[9,3,24,24]{3,2,1,0:T(8,128)(2,1)} %bitcast.14, ...), custom_call_target="tpu_custom_call" | custom-call | flops 20000000000 | bytes 10000000 | tf_op jit(solution)/shard_map/pallas_call | solution.py:285
  49.5 26.7 %all-to-all-done = bf16[32,32,1024]{2,1,0:T(8,128)(2,1)S(1)} async-done(((bf16[32,32,1024]{2,1,0:T(8,128)(2,1)}), bf16[32,32,1024]{2,1,0:T(8,128)(2,1)S(1)}, u32[]{:S(2)}, u32[]{:S(2)}) %all-to-all-start) | async-done | bytes 2097184 | tf_op jit(solution)/shard_map/all_to_all | solution.py:478
  76.2 0.0 copy-start
  76.2 1.3 copy-done
  77.5 0.0 copy-start.5
  77.5 0.0 copy-start.6
  77.5 0.0 copy-start.7
  77.5 11.0 %shard_map.192 = bf16[32,24,256]{2,1,0:T(8,128)(2,1)} custom-call(bf16[1024,1024]{1,0:T(8,128)(2,1)} %bitcast.9, bf16[2048,1024]{1,0:T(8,128)(2,1)} %constant.39.clone.t_ref, f32[2,8,8,16,512]{4,3,2,1,0:T(8,128)} %s_ref.1), custom_call_target="tpu_custom_call" | custom-call | tf_op jit(solution)/shard_map/pallas_call | solution.py:151
  88.5 4.2 %all-to-all-start.1 = ((bf16[32,24,256]{2,1,0:T(8,128)(2,1)}), bf16[32,24,256]{2,1,0:T(8,128)(2,1)S(1)}, u32[]{:S(2)}, u32[]{:S(2)}) async-start(bf16[32,24,256]{2,1,0:T(8,128)(2,1)} %shard_map.192), calls=%async_computation.1 | async-start | bytes 786432 | tf_op jit(solution)/shard_map/all_to_all | solution.py:482
  92.7 0.0 copy-done.5
  92.7 0.1 stack_tile.6
  92.8 0.0 copy-done.6
  92.8 0.1 stack_tile.7
  92.9 0.0 copy-done.7
  92.9 0.1 broadcast_in_dim.3
  93.0 0.7 broadcast_in_dim_reshape.3.b3_ref
  93.7 0.7 pad_add_fusion.place_ref
  94.3 0.6 pad_maximum_fusion.b12_ref
  94.9 10.8 %all-to-all-done.1.in_ref = bf16[32,24,256]{2,1,0:T(8,128)(2,1)S(1)} async-done(((bf16[32,24,256]{2,1,0:T(8,128)(2,1)}), bf16[32,24,256]{2,1,0:T(8,128)(2,1)S(1)}, u32[]{:S(2)}, u32[]{:S(2)}) %all-to-all-start.1) | async-done | bytes 393248 | tf_op jit(solution)/shard_map/all_to_all | solution.py:482
  105.7 0.0 copy-start.1
  105.7 0.7 copy-done.1
  106.5 69.7 %shard_map.193 = bf16[24,16,16,256]{3,2,1,0:T(8,128)(2,1)} custom-call(s32[2]{0:T(128)} %pad_add_fusion.place_ref, bf16[32,24,256]{2,1,0:T(8,128)(2,1)} %copy-done.1, bf16[8,768,384]{2,1,0:T(8,128)(2,1)} %get-tuple-element.19.w1_ref, bf16[2,768,384]{2,1,0:T(8,128)(2,1)} %get-tuple-element.20.w1_side_ref, bf16[2,2304,256]{2,1,0:T(8,128)(2,1)} %get-tuple-element.21.w2_ref, ...), custom_call_target="tpu_custom_call" | custom-call | tf_op jit(solution)/shard_map/pallas_call | solution.py:446
  (2 shorter events, 0.0 us)
Async XLA Ops:
  20.0 7.3 %copy-start.4 = (bf16[24,2,3,3,3]{0,1,4,3,2:T(2,128)(2,1)S(1)}, bf16[24,2,3,3,3]{0,1,4,3,2:T(2,128)(2,1)}, u32[]{:S(2)}) copy-start(bf16[24,2,3,3,3]{0,1,4,3,2:T(2,128)(2,1)} %param.22) | copy-start | bytes 7780
  20.0 8.0 %copy-start.2 = (bf16[24,24,3,3,3]{1,0,4,3,2:T(8,128)(2,1)S(1)}, bf16[24,24,3,3,3]{1,0,4,3,2:T(8,128)(2,1)}, u32[]{:S(2)}) copy-start(bf16[24,24,3,3,3]{1,0,4,3,2:T(8,128)(2,1)} %param.24) | copy-start | bytes 93316
  20.0 8.7 %copy-start.3 = (bf16[24,24,3,3,3]{1,0,4,3,2:T(8,128)(2,1)S(1)}, bf16[24,24,3,3,3]{1,0,4,3,2:T(8,128)(2,1)}, u32[]{:S(2)}) copy-start(bf16[24,24,3,3,3]{1,0,4,3,2:T(8,128)(2,1)} %param.26) | copy-start | bytes 93316
  20.0 56.2 %all-to-all-start = ((bf16[32,32,1024]{2,1,0:T(8,128)(2,1)}), bf16[32,32,1024]{2,1,0:T(8,128)(2,1)S(1)}, u32[]{:S(2)}, u32[]{:S(2)}) async-start(bf16[32,32,1024]{2,1,0:T(8,128)(2,1)} %shard_map.190), calls=%async_computation | async-start | bytes 4194304 | tf_op jit(solution)/shard_map/all_to_all | solution.py:478
  76.2 1.3 copy-start
  77.5 15.2 %copy-start.5 = (f32[24]{0:T(128)S(1)}, f32[24]{0:T(128)}, u32[]{:S(2)}) copy-start(f32[24]{0:T(128)} %param.23) | copy-start | bytes 292
  77.5 15.3 %copy-start.6 = (f32[24]{0:T(128)S(1)}, f32[24]{0:T(128)}, u32[]{:S(2)}) copy-start(f32[24]{0:T(128)} %param.25) | copy-start | bytes 292
  77.5 15.4 %copy-start.7 = (f32[24]{0:T(128)S(1)}, f32[24]{0:T(128)}, u32[]{:S(2)}) copy-start(f32[24]{0:T(128)} %param.27) | copy-start | bytes 292
  88.5 17.2 %all-to-all-start.1 = ((bf16[32,24,256]{2,1,0:T(8,128)(2,1)}), bf16[32,24,256]{2,1,0:T(8,128)(2,1)S(1)}, u32[]{:S(2)}, u32[]{:S(2)}) async-start(bf16[32,24,256]{2,1,0:T(8,128)(2,1)} %shard_map.192), calls=%async_computation.1 | async-start | bytes 786432 | tf_op jit(solution)/shard_map/all_to_all | solution.py:482
  105.7 0.8 copy-start.1

commit v2 on v1

--- a/solution.py
+++ b/solution.py
@@ -13,6 +13,12 @@
 F32 = jnp.float32
 HALO = 3
 WINDOW = 256
+Y_GROUP = 4
+Y_PASSES = 2
+Z_PASSES = 1
+Z_WIDTH = 256
+SECOND_GROUP = 3
+THIRD_GROUP = 4
 VMEM_LIMIT = 56 * 1024 * 1024
 
 
@@ -59,24 +65,33 @@
 
 
 def y_kernel(devices, k_ref, t_ref, out_ref, lines, turned, sems):
-    pairs, kz_here, width = lines.shape[1], lines.shape[0], lines.shape[2]
+    kz_here, pairs, _ = lines.shape
     rows = t_ref.shape[0]
+    group = Y_GROUP
 
     def fetch(kz):
         return pltpu.make_async_copy(k_ref.at[:, kz, :], lines.at[kz], sems.at[kz])
 
     for kz in range(kz_here):
         fetch(kz).start()
-    for kz in range(kz_here):
-        fetch(kz).wait()
-        line = lines[kz]
+    for first in range(0, kz_here, group):
+        for kz in range(first, first + group):
+            fetch(kz).wait()
+        line = lines[first : first + group].reshape(group * pairs, lines.shape[2])
         high = line.astype(BF16)
-        low = (line - high.astype(F32)).astype(BF16)
-        operand = jnp.concatenate([high, high, low], axis=1)
+        terms = [high]
+        if Y_PASSES > 1:
+            terms.append(high)
+        if Y_PASSES > 2:
+            terms.append((line - high.astype(F32)).astype(BF16))
+        operand = jnp.concatenate(terms, axis=1)
         result = lax.dot_general(
             t_ref[...], operand, (((1,), (1,)), ((), ())), preferred_element_type=F32
         )
-        turned[pl.ds(kz, rows, stride=kz_here), :] = result
+        for i in range(group):
+            turned[pl.ds(first + i, rows, stride=kz_here), :] = result[
+                :, i * pairs : (i + 1) * pairs
+            ]
     block = 2 * kz_here
     for row in range(rows // 2):
         y, device = row // devices, row % devices
@@ -90,7 +105,7 @@
     pairs = coils * xs
     y_count = width // 2
     high, low = halves(y_table(y_count, devices))
-    table = jnp.asarray(np.concatenate([high, low, high], axis=1))
+    table = jnp.asarray(np.concatenate([high, low, high][:Y_PASSES], axis=1))
     return pl.pallas_call(
         functools.partial(y_kernel, devices),
         out_shape=jax.ShapeDtypeStruct((devices, 2 * kz_here, y_count // devices * pairs), BF16),
@@ -105,35 +120,35 @@
     )(kspace.reshape(pairs, kz_here, width), table)
 
 
-def z_kernel(scale, devices, y_here, r_ref, t_ref, s_ref, out_ref, merged, turned):
+def z_kernel(scale, devices, z_here, r_ref, t_ref, s_ref, out_ref, lines, turned):
     step = pl.program_id(0)
-    coils, xs, z_count = s_ref.shape[2:]
-    z_here = z_count // devices
-    lines = r_ref[...].T
-    operand = jnp.concatenate([lines, lines], axis=1)
-    images = jnp.dot(operand, t_ref[...], preferred_element_type=F32)
-    image_re = images[:, :z_count].reshape(coils, xs, z_count)
-    image_im = images[:, z_count:].reshape(coils, xs, z_count)
-    sens_re = s_ref[0, 0]
-    sens_im = s_ref[1, 0]
-    real = jnp.sum(sens_re * image_re + sens_im * image_im, axis=0) * scale
-    imag = jnp.sum(sens_re * image_im - sens_im * image_re, axis=0) * scale
-    base = pl.multiple_of(step * 2 * xs, 2 * xs)
-
-    if merged.shape[0] > y_here * 2 * xs:
-
-        @pl.when(step == 0)
-        def _():
-            merged[...] = jnp.zeros_like(merged)
-
-    merged[pl.ds(base, 2 * xs), :] = jnp.concatenate([real, imag], axis=0)
+    _, y_here, coils, xs, width = s_ref.shape
+    lanes = out_ref.shape[2]
+
+    @pl.when(step == 0)
+    def _():
+        lines[...] = r_ref[...].T
+        turned[...] = jnp.zeros_like(turned)
+
+    operand = lines[...]
+    if Z_PASSES > 1:
+        operand = jnp.concatenate([operand, operand], axis=1)
+    images = jnp.dot(operand, t_ref[0], preferred_element_type=F32)
+    image_re = images[:, :width].reshape(y_here, coils, xs, width)
+    image_im = images[:, width:].reshape(y_here, coils, xs, width)
+    sens_re = s_ref[0]
+    sens_im = s_ref[1]
+    real = jnp.sum(sens_re * image_re + sens_im * image_im, axis=1) * scale
+    imag = jnp.sum(sens_re * image_im - sens_im * image_re, axis=1) * scale
+    merged = jnp.concatenate([real, imag], axis=1).reshape(y_here * 2 * xs, width)
+    if lanes > y_here * 2 * xs:
+        merged = jnp.concatenate([merged, jnp.zeros((lanes - y_here * 2 * xs, width), F32)], axis=0)
+    base = pl.multiple_of(8 + step * width, 8)
+    turned[pl.ds(base, width), :] = merged.T
 
     @pl.when(step == pl.num_programs(0) - 1)
     def _():
-        lanes = merged.shape[0]
         rows = out_ref.shape[1]
-        turned[...] = jnp.zeros_like(turned)
-        turned[8 : 8 + z_count, :] = merged[...].T
         for device in range(devices):
             first = 8 + device * z_here - HALO
             out_ref[device] = turned[first : first + rows, :].astype(BF16)
@@ -142,24 +157,28 @@
 def z_transform(received, sensitivity, devices):
     _, y_here, coils, xs, z_count = sensitivity.shape
     pairs = coils * xs
+    width = Z_WIDTH
     high, low = halves(z_table(z_count, devices))
-    table = jnp.asarray(np.concatenate([high, low], axis=0))
+    table = np.concatenate([high, low][:Z_PASSES], axis=0)
+    depth = table.shape[0]
+    table = table.reshape(depth, 2, z_count // width, width).transpose(2, 0, 1, 3)
+    table = jnp.asarray(table.reshape(z_count // width, depth, 2 * width))
     scale = 1.0 / math.sqrt(z_count)
     rows = round_up(z_count // devices + 2 * HALO, 8)
     lanes = round_up(y_here * 2 * xs, 128)
     flat = received.reshape(2 * z_count, y_here * pairs)
     return pl.pallas_call(
-        functools.partial(z_kernel, scale, devices, y_here),
+        functools.partial(z_kernel, scale, devices, z_count // devices),
         out_shape=jax.ShapeDtypeStruct((devices, rows, lanes), BF16),
-        grid=(y_here,),
+        grid=(z_count // width,),
         in_specs=[
-            pl.BlockSpec((2 * z_count, pairs), lambda y: (0, y)),
-            pl.BlockSpec(table.shape, lambda y: (0, 0)),
-            pl.BlockSpec((2, 1, coils, xs, z_count), lambda y: (0, y, 0, 0, 0)),
+            pl.BlockSpec(flat.shape, lambda z: (0, 0)),
+            pl.BlockSpec((1, depth, 2 * width), lambda z: (z, 0, 0)),
+            pl.BlockSpec((2, y_here, coils, xs, width), lambda z: (0, 0, 0, 0, z)),
         ],
-        out_specs=pl.BlockSpec((devices, rows, lanes), lambda y: (0, 0, 0)),
+        out_specs=pl.BlockSpec((devices, rows, lanes), lambda z: (0, 0, 0)),
         scratch_shapes=[
-            pltpu.VMEM((lanes, z_count), F32),
+            pltpu.VMEM(flat.shape[::-1], BF16),
             pltpu.VMEM((8 + z_count + 32, lanes), F32),
         ],
         compiler_params=params(),
@@ -346,17 +365,14 @@
     window = 256
     lanes = act1.shape[3]
 
-    def taps(act, z, h):
+    def taps(act, z, count, h):
         start = h * (lanes - window)
         pieces = []
         for dz in range(3):
             for dy in range(3):
-                piece = act[z + dz, dy : dy + y_here, :, start : start + window]
-                pieces.append(piece.reshape(y_here * devices, window))
+                piece = act[pl.ds(z + dz, count), dy : dy + y_here, :, start : start + window]
+                pieces.append(piece.reshape(count * y_here * devices, window))
         return jnp.concatenate(pieces, axis=1)
-
-    def inside(z):
-        return jnp.where((z >= 0) & (z < z_count), 1.0, 0.0).astype(F32)
 
     @pl.when(pl.program_id(0) == 0)
     def _():
@@ -377,56 +393,72 @@
 
         lax.fori_loop(0, z1 + 2, shift, 0)
 
-        def first(z, carry):
-            def three(ref):
-                pieces = []
-                for dz in range(3):
-                    base = pl.multiple_of((z + dz) * devices, devices)
-                    pieces.append(ref[pl.ds(base, devices), :])
-                return jnp.concatenate(pieces, axis=1)
-
-            mask = inside(first_z + z - 2)
-            middle = three(own)
-            for m in range(y_here):
-                result = jnp.dot(middle, w1_ref[m], preferred_element_type=F32)
+        def three(ref):
+            count = z1 * devices
+            return jnp.concatenate(
+                [ref[dz * devices : dz * devices + count, :] for dz in range(3)], axis=1
+            )
+
+        for m in range(y_here):
+            result = jnp.dot(three(own), w1_ref[m], preferred_element_type=F32)
+            if m == 0:
+                result += jnp.dot(three(before), w1_side_ref[0], preferred_element_type=F32)
+            if m == y_here - 1:
+                result += jnp.dot(three(after), w1_side_ref[1], preferred_element_type=F32)
+            value = jnp.maximum(result + b12_ref[0:1, :], 0.0).reshape(z1, devices, lanes)
+            act1[:, m + 1] = value.astype(BF16)
+            for z in range(z1):
                 if m == 0:
-                    result += jnp.dot(three(before), w1_side_ref[0], preferred_element_type=F32)
+                    act1[z, groups - 1] = up_one(value[z]).astype(BF16)
                 if m == y_here - 1:
-                    result += jnp.dot(three(after), w1_side_ref[1], preferred_element_type=F32)
-                value = jnp.maximum(result + b12_ref[0:1, :], 0.0) * mask
-                act1[z, m + 1] = value.astype(BF16)
-                if m == 0:
-                    act1[z, groups - 1] = up_one(value).astype(BF16)
-                if m == y_here - 1:
-                    act1[z, 0] = down_one(value).astype(BF16)
+                    act1[z, 0] = down_one(value[z]).astype(BF16)
+        for z in (0, 1, z1 - 2, z1 - 1):
+            here = first_z + z - 2
+
+            @pl.when((here < 0) | (here >= z_count))
+            def _():
+                act1[z] = jnp.zeros_like(act1[z])
+
+        many = SECOND_GROUP
+
+        def second(step, carry):
+            z = step * many
+            left = jnp.dot(taps(act1, z, many, 0), w2_ref[0], preferred_element_type=F32)
+            right = jnp.dot(taps(act1, z, many, 1), w2_ref[1], preferred_element_type=F32)
+            value = jnp.maximum(join(left, right) + b12_ref[1:2, :], 0.0)
+            cube = value.reshape(many, y_here, devices, lanes)
+            act2[pl.ds(z, many), 1 : groups - 1] = cube.astype(BF16)
+            for i in range(many):
+                act2[z + i, groups - 1] = up_one(cube[i, 0]).astype(BF16)
+                act2[z + i, 0] = down_one(cube[i, y_here - 1]).astype(BF16)
             return carry
 
-        lax.fori_loop(0, z1, first, 0)
-
-        def second(z, carry):
-            left = jnp.dot(taps(act1, z, 0), w2_ref[0], preferred_element_type=F32)
-            right = jnp.dot(taps(act1, z, 1), w2_ref[1], preferred_element_type=F32)
-            mask = inside(first_z + z - 1)
-            value = jnp.maximum(join(left, right) + b12_ref[1:2, :], 0.0) * mask
-            cube = value.reshape(y_here, devices, lanes)
-            act2[z, 1 : groups - 1] = cube.astype(BF16)
-            act2[z, groups - 1] = up_one(cube[0]).astype(BF16)
-            act2[z, 0] = down_one(cube[y_here - 1]).astype(BF16)
-            return carry
-
-        lax.fori_loop(0, z2, second, 0)
-
-    z = pl.program_id(0)
-    channels, _, xs, y_count = out_ref.shape
+        lax.fori_loop(0, z2 // many, second, 0)
+        for z in (0, z2 - 1):
+            here = first_z + z - 1
+
+            @pl.when((here < 0) | (here >= z_count))
+            def _():
+                act2[z] = jnp.zeros_like(act2[z])
+
+    channels, many, xs, y_count = out_ref.shape
+    z = pl.program_id(0) * many
     parts = []
     for h in range(2):
-        result = jnp.dot(taps(act2, z, h), w3_ref[h], preferred_element_type=F32)
+        result = jnp.dot(taps(act2, z, many, h), w3_ref[h], preferred_element_type=F32)
         value = jnp.maximum(result + b3_ref[...], 0.0).astype(BF16)
-        turned = lax.dot_general(
-            value, order_ref[...], (((0,), (0,)), ((), ())), preferred_element_type=F32
-        )
-        parts.append(turned.reshape(channels, xs // 2, y_count))
-    out_ref[:, 0] = jnp.concatenate(parts, axis=1).astype(BF16)
+        parts.append(value)
+    for i in range(many):
+        pieces = []
+        for value in parts:
+            turned = lax.dot_general(
+                value[i * y_count : (i + 1) * y_count],
+                order_ref[...],
+                (((0,), (0,)), ((), ())),
+                preferred_element_type=F32,
+            )
+            pieces.append(turned.reshape(channels, xs // 2, y_count))
+        out_ref[:, i] = jnp.concatenate(pieces, axis=1).astype(BF16)
 
 
 def network(gathered, place, weights, biases, z_here, xs, y_here):
@@ -446,9 +478,9 @@
     return pl.pallas_call(
         net_kernel,
         out_shape=jax.ShapeDtypeStruct((channels, z_here, xs, y_count), BF16),
-        grid=(z_here,),
+        grid=(z_here // THIRD_GROUP,),
         in_specs=[pl.BlockSpec(memory_space=pltpu.SMEM)] + [vmem_spec()] * 8,
-        out_specs=pl.BlockSpec((channels, 1, xs, y_count), lambda z: (0, z, 0, 0)),
+        out_specs=pl.BlockSpec((channels, THIRD_GROUP, xs, y_count), lambda z: (0, z, 0, 0)),
         scratch_shapes=[
             pltpu.VMEM((lanes_in // 128, rows_in * devices, 128), F32),
             pltpu.VMEM((rows_in * devices, lanes_in), BF16),

time: 177 us -> 126 us (0.71)
  Pallas kernels: 121 us -> 69.9 us
    pallas_call x1, Pallas kernels: 69.7 us -> 35 us  [network(): pl.pallas_call(net_kernel, out_shape=jax.ShapeDtypeStruct((channels, z_he...]
    pallas_call x1, Pallas kernels: 20 us -> 8.15 us  [y_transform(): pl.pallas_call(functools.partial(y_kernel, devices), out_shape=jax.ShapeD...]
    pallas_call x1, Pallas kernels: 11 us -> 6.85 us  [z_transform(): pl.pallas_call(functools.partial(z_kernel, scale, devices, z_count // dev...]
  transfers between devices with their start and end apart: 2 -> 2, of which waited for: 2 -> 2; matrix products, arithmetic and copies ran while one was open for 2% -> 3% of each run, Pallas kernels for 11% -> 16%
where the time goes in v2:
time: 126 us; the launch traced here: 125 us
  Pallas kernels  69.9 us (55%)
  waiting for transfers between devices  37.5 us (30%)
  starting transfers between devices  11.5 us (9%)
  local copies, waits for them, and re-layouts  5.24 us (4%)
    pallas_call x1, Pallas kernels, network(): pl.pallas_call(net_kernel, out_shape=jax.ShapeDtypeStruct((channels, z_he...  35 us
    all_to_all x1, waiting for transfers between devices, on_device(): received = lax.all_to_all(lines, 'kz', 0, 0)  26.7 us
    pallas_call x1, Pallas kernels, expand_weights(): pl.pallas_call(functools.partial(expand_kernel, y_here), out_shape=(jax.S...  19.9 us
    all_to_all x1, waiting for transfers between devices, on_device(): gathered = lax.all_to_all(merged, 'kz', 0, 0)  10.8 us
    pallas_call x1, Pallas kernels, y_transform(): pl.pallas_call(functools.partial(y_kernel, devices), out_shape=jax.ShapeD...  8.15 us
    all_to_all x1, starting transfers between devices, on_device(): received = lax.all_to_all(lines, 'kz', 0, 0)  7.3 us
    pallas_call x1, Pallas kernels, z_transform(): pl.pallas_call(functools.partial(z_kernel, scale, devices, z_count // dev...  6.85 us
    all_to_all x1, starting transfers between devices, on_device(): gathered = lax.all_to_all(merged, 'kz', 0, 0)  4.19 us
  transfers between devices with their start and end apart: 2, of which 2 were waited for; matrix products, arithmetic and copies ran while one was open for 3% of the time, Pallas kernels for 16%

profile of v2, /device:TPU:0, one launch (start us, length us, event | category | flops | bytes accessed | tf_op | source)
XLA Modules:
  0.0 125.5 jit_solution(8843867207114586135)
XLA Ops:
  0.0 8.1 %shard_map.190 = bf16[32,32,1024]{2,1,0:T(8,128)(2,1)} custom-call(f32[128,16,512]{2,1,0:T(8,128)} %bitcast.10, bf16[512,1024]{1,0:T(8,128)(2,1)} %constant.30.clone.t_ref), custom_call_target="tpu_custom_call" | custom-call | tf_op jit(solution)/shard_map/pallas_call | solution.py:109
  8.2 0.0 copy-start.4
  8.2 0.0 copy-start.2
  8.2 0.0 copy-start.3
  8.2 7.3 %all-to-all-start = ((bf16[32,32,1024]{2,1,0:T(8,128)(2,1)}), bf16[32,32,1024]{2,1,0:T(8,128)(2,1)S(1)}, u32[]{:S(2)}, u32[]{:S(2)}) async-start(bf16[32,32,1024]{2,1,0:T(8,128)(2,1)} %shard_map.190), calls=%async_computation | async-start | bytes 4194304 | tf_op jit(solution)/shard_map/all_to_all | solution.py:510
  15.5 0.0 copy-done.4
  15.5 0.6 copy.24
  16.1 0.0 copy-done.2
  16.1 0.8 copy.25
  16.9 0.0 copy-done.3
  16.9 0.8 copy.26
  17.7 19.9 %shard_map.191 = (bf16[8,768,384]{2,1,0:T(8,128)(2,1)}, bf16[2,768,384]{2,1,0:T(8,128)(2,1)}, bf16[2,2304,256]{2,1,0:T(8,128)(2,1)}, bf16[2,2304,192]{2,1,0:T(8,128)(2,1)}) custom-call(bf16[9,3,2,24]{3,2,1,0:T(2,128)(2,1)} %bitcast.16, bf16[9,3,24,24]{3,2,1,0:T(8,128)(2,1)} %bitcast.13, bf16[9,3,24,24]{3,2,1,0:T(8,128)(2,1)} %bitcast.14, ...), custom_call_target="tpu_custom_call" | custom-call | flops 20000000000 | bytes 10000000 | tf_op jit(solution)/shard_map/pallas_call | solution.py:304
  37.7 26.7 %all-to-all-done = bf16[32,32,1024]{2,1,0:T(8,128)(2,1)S(1)} async-done(((bf16[32,32,1024]{2,1,0:T(8,128)(2,1)}), bf16[32,32,1024]{2,1,0:T(8,128)(2,1)S(1)}, u32[]{:S(2)}, u32[]{:S(2)}) %all-to-all-start) | async-done | bytes 2097184 | tf_op jit(solution)/shard_map/all_to_all | solution.py:510
  64.4 0.0 copy-start
  64.4 1.3 %copy-done = bf16[32,32,1024]{2,1,0:T(8,128)(2,1)} copy-done((bf16[32,32,1024]{2,1,0:T(8,128)(2,1)}, bf16[32,32,1024]{2,1,0:T(8,128)(2,1)S(1)}, u32[]{:S(2)}) %copy-start) | copy-done | bytes 2097176
  65.7 0.0 copy-start.5
  65.7 0.0 copy-start.6
  65.7 0.0 copy-start.7
  65.7 6.9 %shard_map.192 = bf16[32,24,256]{2,1,0:T(8,128)(2,1)} custom-call(bf16[1024,1024]{1,0:T(8,128)(2,1)} %bitcast.9, bf16[2,1024,512]{2,1,0:T(8,128)(2,1)} %constant.39.clone.t_ref, f32[2,8,8,16,512]{4,3,2,1,0:T(8,128)} %s_ref.1), custom_call_target="tpu_custom_call" | custom-call | tf_op jit(solution)/shard_map/pallas_call | solution.py:170
  72.6 4.2 %all-to-all-start.1 = ((bf16[32,24,256]{2,1,0:T(8,128)(2,1)}), bf16[32,24,256]{2,1,0:T(8,128)(2,1)S(1)}, u32[]{:S(2)}, u32[]{:S(2)}) async-start(bf16[32,24,256]{2,1,0:T(8,128)(2,1)} %shard_map.192), calls=%async_computation.1 | async-start | bytes 786432 | tf_op jit(solution)/shard_map/all_to_all | solution.py:514
  76.8 0.0 copy-done.5
  76.8 0.1 stack_tile.6
  76.9 0.0 copy-done.6
  76.9 0.1 stack_tile.7
  77.0 0.0 copy-done.7
  77.0 0.1 broadcast_in_dim.3
  77.1 0.7 broadcast_in_dim_reshape.3.b3_ref
  77.8 0.7 pad_add_fusion.place_ref
  78.4 0.6 pad_maximum_fusion.b12_ref
  79.0 10.8 %all-to-all-done.1.in_ref = bf16[32,24,256]{2,1,0:T(8,128)(2,1)S(1)} async-done(((bf16[32,24,256]{2,1,0:T(8,128)(2,1)}), bf16[32,24,256]{2,1,0:T(8,128)(2,1)S(1)}, u32[]{:S(2)}, u32[]{:S(2)}) %all-to-all-start.1) | async-done | bytes 393248 | tf_op jit(solution)/shard_map/all_to_all | solution.py:514
  89.8 0.0 copy-start.1
  89.8 0.7 copy-done.1
  90.5 35.0 %shard_map.193 = bf16[24,16,16,256]{3,2,1,0:T(8,128)(2,1)} custom-call(s32[2]{0:T(128)} %pad_add_fusion.place_ref, bf16[32,24,256]{2,1,0:T(8,128)(2,1)} %copy-done.1, bf16[8,768,384]{2,1,0:T(8,128)(2,1)} %get-tuple-element.19.w1_ref, bf16[2,768,384]{2,1,0:T(8,128)(2,1)} %get-tuple-element.20.w1_side_ref, bf16[2,2304,256]{2,1,0:T(8,128)(2,1)} %get-tuple-element.21.w2_ref, ...), custom_call_target="tpu_custom_call" | custom-call | tf_op jit(solution)/shard_map/pallas_call | solution.py:478
  (2 shorter events, 0.0 us)
Async XLA Ops:
  8.2 7.3 %copy-start.4 = (bf16[24,2,3,3,3]{0,1,4,3,2:T(2,128)(2,1)S(1)}, bf16[24,2,3,3,3]{0,1,4,3,2:T(2,128)(2,1)}, u32[]{:S(2)}) copy-start(bf16[24,2,3,3,3]{0,1,4,3,2:T(2,128)(2,1)} %param.22) | copy-start | bytes 7780
  8.2 8.0 %copy-start.2 = (bf16[24,24,3,3,3]{1,0,4,3,2:T(8,128)(2,1)S(1)}, bf16[24,24,3,3,3]{1,0,4,3,2:T(8,128)(2,1)}, u32[]{:S(2)}) copy-start(bf16[24,24,3,3,3]{1,0,4,3,2:T(8,128)(2,1)} %param.24) | copy-start | bytes 93316
  8.2 8.7 %copy-start.3 = (bf16[24,24,3,3,3]{1,0,4,3,2:T(8,128)(2,1)S(1)}, bf16[24,24,3,3,3]{1,0,4,3,2:T(8,128)(2,1)}, u32[]{:S(2)}) copy-start(bf16[24,24,3,3,3]{1,0,4,3,2:T(8,128)(2,1)} %param.26) | copy-start | bytes 93316
  8.2 56.2 %all-to-all-start = ((bf16[32,32,1024]{2,1,0:T(8,128)(2,1)}), bf16[32,32,1024]{2,1,0:T(8,128)(2,1)S(1)}, u32[]{:S(2)}, u32[]{:S(2)}) async-start(bf16[32,32,1024]{2,1,0:T(8,128)(2,1)} %shard_map.190), calls=%async_computation | async-start | bytes 4194304 | tf_op jit(solution)/shard_map/all_to_all | solution.py:510
  64.4 1.3 %copy-start = (bf16[32,32,1024]{2,1,0:T(8,128)(2,1)}, bf16[32,32,1024]{2,1,0:T(8,128)(2,1)S(1)}, u32[]{:S(2)}) copy-start(bf16[32,32,1024]{2,1,0:T(8,128)(2,1)S(1)} %all-to-all-done) | copy-start | bytes 6291460
  65.7 11.1 %copy-start.5 = (f32[24]{0:T(128)S(1)}, f32[24]{0:T(128)}, u32[]{:S(2)}) copy-start(f32[24]{0:T(128)} %param.23) | copy-start | bytes 292
  65.7 11.2 %copy-start.6 = (f32[24]{0:T(128)S(1)}, f32[24]{0:T(128)}, u32[]{:S(2)}) copy-start(f32[24]{0:T(128)} %param.25) | copy-start | bytes 292
  65.7 11.3 %copy-start.7 = (f32[24]{0:T(128)S(1)}, f32[24]{0:T(128)}, u32[]{:S(2)}) copy-start(f32[24]{0:T(128)} %param.27) | copy-start | bytes 292
  72.6 17.2 %all-to-all-start.1 = ((bf16[32,24,256]{2,1,0:T(8,128)(2,1)}), bf16[32,24,256]{2,1,0:T(8,128)(2,1)S(1)}, u32[]{:S(2)}, u32[]{:S(2)}) async-start(bf16[32,24,256]{2,1,0:T(8,128)(2,1)} %shard_map.192), calls=%async_computation.1 | async-start | bytes 786432 | tf_op jit(solution)/shard_map/all_to_all | solution.py:514
  89.8 0.8 copy-start.1

commit v3 on v2

--- a/solution.py
+++ b/solution.py
@@ -14,9 +14,9 @@
 HALO = 3
 WINDOW = 256
 Y_GROUP = 4
-Y_PASSES = 2
-Z_PASSES = 1
-Z_WIDTH = 256
+Y_PASSES = 3
+Z_WIDTH = 128
+CODE_SCALE = 2.0**20
 SECOND_GROUP = 3
 THIRD_GROUP = 4
 VMEM_LIMIT = 56 * 1024 * 1024
@@ -44,6 +44,10 @@
     phase = (rows[:, None] * cols[None, :]) % length
     angle = phase * (2.0 * math.pi / length)
     return np.cos(angle), np.sin(angle)
+
+
+def parities(kz_here):
+    return 2 if kz_here % 16 == 0 else 1
 
 
 def y_table(y_count, devices):
@@ -52,22 +56,39 @@
     cosine, sine = trig(y_count, order, np.arange(y_count))
     real = np.concatenate([cosine, -sine], axis=1)
     imag = np.concatenate([sine, cosine], axis=1)
-    table = np.stack([real, imag], axis=1).reshape(2 * y_count, 2 * y_count)
-    return table / math.sqrt(y_count)
-
-
-def z_table(z_count, devices):
-    cosine, sine = trig(z_count, np.arange(z_count), np.arange(z_count))
-    real = np.concatenate([cosine, sine], axis=1)
-    imag = np.concatenate([-sine, cosine], axis=1)
-    table = np.stack([real, imag], axis=0).reshape(2, devices, z_count // devices, 2 * z_count)
-    return np.transpose(table, (1, 0, 2, 3)).reshape(2 * z_count, 2 * z_count)
+    return np.concatenate([real, imag], axis=0) * (CODE_SCALE / math.sqrt(y_count))
+
+
+def z_table(z_count, devices, groups, width):
+    kz_here = z_count // devices
+    outputs = z_count // groups
+    tables = []
+    for parity in range(groups):
+        kz = np.arange(devices)[:, None] * kz_here + np.arange(parity, kz_here, groups)[None, :]
+        cosine, sine = trig(z_count, kz.reshape(-1), np.arange(outputs))
+        both = np.stack([np.stack([cosine, sine], 1), np.stack([-sine, cosine], 1)], 0)
+        both = both.reshape(2, devices, kz_here // groups, 2, outputs // width, width)
+        both = both.transpose(4, 1, 0, 2, 3, 5)
+        tables.append(both.reshape(outputs // width, 2 * z_count // groups, 2 * width))
+    return np.stack(tables)
+
+
+def encode(value):
+    square = value * jnp.abs(value)
+    return (square * jnp.abs(square)).astype(BF16)
+
+
+def decode(code):
+    code = code.astype(F32)
+    root = jnp.sqrt(jnp.sqrt(jnp.abs(code)))
+    return jnp.where(code < 0, -root, root)
 
 
 def y_kernel(devices, k_ref, t_ref, out_ref, lines, turned, sems):
     kz_here, pairs, _ = lines.shape
     rows = t_ref.shape[0]
-    group = Y_GROUP
+    group = min(Y_GROUP, kz_here)
+    groups = parities(kz_here)
 
     def fetch(kz):
         return pltpu.make_async_copy(k_ref.at[:, kz, :], lines.at[kz], sems.at[kz])
@@ -88,16 +109,21 @@
         result = lax.dot_general(
             t_ref[...], operand, (((1,), (1,)), ((), ())), preferred_element_type=F32
         )
+        block = 2 * kz_here
+        half = rows // 2
         for i in range(group):
-            turned[pl.ds(first + i, rows, stride=kz_here), :] = result[
-                :, i * pairs : (i + 1) * pairs
-            ]
-    block = 2 * kz_here
+            kz = first + i
+            for part in range(2):
+                place = kz % groups * (block // groups)
+                place += part * (kz_here // groups) + kz // groups
+                turned[pl.ds(place, half, stride=block), :] = result[
+                    part * half : (part + 1) * half, i * pairs : (i + 1) * pairs
+                ]
     for row in range(rows // 2):
         y, device = row // devices, row % devices
-        out_ref[device, :, y * pairs : (y + 1) * pairs] = turned[
-            row * block : (row + 1) * block, :
-        ].astype(BF16)
+        out_ref[device, :, y * pairs : (y + 1) * pairs] = encode(
+            turned[row * block : (row + 1) * block, :]
+        )
 
 
 def y_transform(kspace, devices):
@@ -120,69 +146,97 @@
     )(kspace.reshape(pairs, kz_here, width), table)
 
 
-def z_kernel(scale, devices, z_here, r_ref, t_ref, s_ref, out_ref, lines, turned):
+def z_kernel(scale, devices, z_here, groups, r_ref, t_ref, *refs):
+    s_refs, out_ref, codes, lines, turned = refs[:groups], *refs[groups:]
     step = pl.program_id(0)
-    _, y_here, coils, xs, width = s_ref.shape
+    _, y_here, coils, xs, width = s_refs[0].shape
     lanes = out_ref.shape[2]
+    columns = r_ref.shape[2]
+    rows = r_ref.shape[1] // groups
+    depth = devices * rows
 
     @pl.when(step == 0)
     def _():
-        lines[...] = r_ref[...].T
+        for parity in range(groups):
+            piece = r_ref[:, parity * rows : (parity + 1) * rows, :]
+            codes[parity] = piece.reshape(depth, columns).T
         turned[...] = jnp.zeros_like(turned)
 
-    operand = lines[...]
-    if Z_PASSES > 1:
-        operand = jnp.concatenate([operand, operand], axis=1)
-    images = jnp.dot(operand, t_ref[0], preferred_element_type=F32)
-    image_re = images[:, :width].reshape(y_here, coils, xs, width)
-    image_im = images[:, width:].reshape(y_here, coils, xs, width)
-    sens_re = s_ref[0]
-    sens_im = s_ref[1]
-    real = jnp.sum(sens_re * image_re + sens_im * image_im, axis=1) * scale
-    imag = jnp.sum(sens_re * image_im - sens_im * image_re, axis=1) * scale
-    merged = jnp.concatenate([real, imag], axis=1).reshape(y_here * 2 * xs, width)
-    if lanes > y_here * 2 * xs:
-        merged = jnp.concatenate([merged, jnp.zeros((lanes - y_here * 2 * xs, width), F32)], axis=0)
-    base = pl.multiple_of(8 + step * width, 8)
-    turned[pl.ds(base, width), :] = merged.T
+        def unpack(i, carry):
+            at = pl.ds(pl.multiple_of(i * 32, 32), 32)
+            for parity in range(groups):
+                value = decode(codes[parity, at, :])
+                high = value.astype(BF16)
+                lines[parity, at, :depth] = high
+                lines[parity, at, depth:] = (value - high.astype(F32)).astype(BF16)
+            return carry
+
+        lax.fori_loop(0, columns // 32, unpack, 0)
+
+    products = []
+    for parity in range(groups):
+        operand = lines[parity]
+        operand = jnp.concatenate([operand, operand[:, :depth]], axis=1)
+        products.append(jnp.dot(operand, t_ref[parity, 0], preferred_element_type=F32))
+    if groups == 2:
+        products = [products[0] + products[1], products[0] - products[1]]
+    for part, (images, s_ref) in enumerate(zip(products, s_refs)):
+        image_re = images[:, :width].reshape(y_here, coils, xs, width)
+        image_im = images[:, width:].reshape(y_here, coils, xs, width)
+        sens_re = s_ref[0]
+        sens_im = s_ref[1]
+        real = jnp.sum(sens_re * image_re + sens_im * image_im, axis=1) * scale
+        imag = jnp.sum(sens_re * image_im - sens_im * image_re, axis=1) * scale
+        merged = jnp.concatenate([real, imag], axis=1).reshape(y_here * 2 * xs, width)
+        extra = lanes - y_here * 2 * xs
+        if extra:
+            merged = jnp.concatenate([merged, jnp.zeros((extra, width), F32)], axis=0)
+        base = 8 + part * devices * z_here // groups
+        base = pl.multiple_of(base + step * width, 8)
+        turned[pl.ds(base, width), :] = merged.T
 
     @pl.when(step == pl.num_programs(0) - 1)
     def _():
-        rows = out_ref.shape[1]
         for device in range(devices):
             first = 8 + device * z_here - HALO
-            out_ref[device] = turned[first : first + rows, :].astype(BF16)
+            out_ref[device] = turned[first : first + out_ref.shape[1], :].astype(BF16)
 
 
 def z_transform(received, sensitivity, devices):
     _, y_here, coils, xs, z_count = sensitivity.shape
     pairs = coils * xs
     width = Z_WIDTH
-    high, low = halves(z_table(z_count, devices))
-    table = np.concatenate([high, low][:Z_PASSES], axis=0)
-    depth = table.shape[0]
-    table = table.reshape(depth, 2, z_count // width, width).transpose(2, 0, 1, 3)
-    table = jnp.asarray(table.reshape(z_count // width, depth, 2 * width))
-    scale = 1.0 / math.sqrt(z_count)
+    groups = parities(z_count // devices)
+    high, low = halves(z_table(z_count, devices, groups, width))
+    table = jnp.asarray(np.concatenate([high, high, low], axis=2))
+    scale = 1.0 / (math.sqrt(z_count) * CODE_SCALE)
     rows = round_up(z_count // devices + 2 * HALO, 8)
     lanes = round_up(y_here * 2 * xs, 128)
-    flat = received.reshape(2 * z_count, y_here * pairs)
+    steps = z_count // groups // width
+    depth = 2 * z_count // groups
+
+    def sens_spec(part):
+        return pl.BlockSpec(
+            (2, y_here, coils, xs, width), lambda z: (0, 0, 0, 0, z + part * steps)
+        )
+
     return pl.pallas_call(
-        functools.partial(z_kernel, scale, devices, z_count // devices),
+        functools.partial(z_kernel, scale, devices, z_count // devices, groups),
         out_shape=jax.ShapeDtypeStruct((devices, rows, lanes), BF16),
-        grid=(z_count // width,),
+        grid=(steps,),
         in_specs=[
-            pl.BlockSpec(flat.shape, lambda z: (0, 0)),
-            pl.BlockSpec((1, depth, 2 * width), lambda z: (z, 0, 0)),
-            pl.BlockSpec((2, y_here, coils, xs, width), lambda z: (0, 0, 0, 0, z)),
-        ],
+            pl.BlockSpec(received.shape, lambda z: (0, 0, 0)),
+            pl.BlockSpec((groups, 1, 3 * depth, 2 * width), lambda z: (0, z, 0, 0)),
+        ]
+        + [sens_spec(part) for part in range(groups)],
         out_specs=pl.BlockSpec((devices, rows, lanes), lambda z: (0, 0, 0)),
         scratch_shapes=[
-            pltpu.VMEM(flat.shape[::-1], BF16),
+            pltpu.VMEM((groups, y_here * pairs, depth), BF16),
+            pltpu.VMEM((groups, y_here * pairs, 2 * depth), BF16),
             pltpu.VMEM((8 + z_count + 32, lanes), F32),
         ],
         compiler_params=params(),
-    )(flat, table, sensitivity)
+    )(received, table, *[sensitivity] * groups)
 
 
 def window_starts(lanes):

time: 126 us -> 133 us (1.056)
  Pallas kernels: 69.9 us -> 77.3 us
    pallas_call x1, Pallas kernels: 6.85 us -> 11.6 us  [z_transform(): pl.pallas_call(functools.partial(z_kernel, scale, devices, z_count // dev...]
    pallas_call x1, Pallas kernels: 8.15 us -> 10.8 us  [y_transform(): pl.pallas_call(functools.partial(y_kernel, devices), out_shape=jax.ShapeD...]
  transfers between devices with their start and end apart: 2 -> 2, of which waited for: 2 -> 2; matrix products, arithmetic and copies ran while one was open for 3% -> 3% of each run, Pallas kernels for 16% -> 15%
where the time goes in v3:
time: 133 us
  Pallas kernels  77.3 us (58%)
  waiting for transfers between devices  37.5 us (28%)
  starting transfers between devices  11.5 us (9%)
  local copies, waits for them, and re-layouts  5.24 us (4%)
    pallas_call x1, Pallas kernels, network(): pl.pallas_call(net_kernel, out_shape=jax.ShapeDtypeStruct((channels, z_he...  35 us
    all_to_all x1, waiting for transfers between devices, on_device(): received = lax.all_to_all(lines, 'kz', 0, 0)  26.7 us
    pallas_call x1, Pallas kernels, expand_weights(): pl.pallas_call(functools.partial(expand_kernel, y_here), out_shape=(jax.S...  20 us
    pallas_call x1, Pallas kernels, z_transform(): pl.pallas_call(functools.partial(z_kernel, scale, devices, z_count // dev...  11.6 us
    pallas_call x1, Pallas kernels, y_transform(): pl.pallas_call(functools.partial(y_kernel, devices), out_shape=jax.ShapeD...  10.8 us
    all_to_all x1, waiting for transfers between devices, on_device(): gathered = lax.all_to_all(merged, 'kz', 0, 0)  10.8 us
    all_to_all x1, starting transfers between devices, on_device(): received = lax.all_to_all(lines, 'kz', 0, 0)  7.3 us
    all_to_all x1, starting transfers between devices, on_device(): gathered = lax.all_to_all(merged, 'kz', 0, 0)  4.19 us
  transfers between devices with their start and end apart: 2, of which 2 were waited for; matrix products, arithmetic and copies ran while one was open for 3% of the time, Pallas kernels for 15%

profile of v3, /device:TPU:0, one launch (start us, length us, event | category | flops | bytes accessed | tf_op | source)
XLA Modules:
  0.0 132.9 jit_solution(7629931922293361763)
XLA Ops:
  0.0 10.8 %shard_map.190 = bf16[32,32,1024]{2,1,0:T(8,128)(2,1)} custom-call(f32[128,16,512]{2,1,0:T(8,128)} %bitcast.8, bf16[512,1536]{1,0:T(8,128)(2,1)} %constant.30.clone.t_ref), custom_call_target="tpu_custom_call" | custom-call | tf_op jit(solution)/shard_map/pallas_call | solution.py:135
  10.8 0.0 copy-start.4
  10.8 0.0 copy-start.2
  10.8 0.0 copy-start.3
  10.8 7.3 %all-to-all-start = ((bf16[32,32,1024]{2,1,0:T(8,128)(2,1)}), bf16[32,32,1024]{2,1,0:T(8,128)(2,1)S(1)}, u32[]{:S(2)}, u32[]{:S(2)}) async-start(bf16[32,32,1024]{2,1,0:T(8,128)(2,1)} %shard_map.190), calls=%async_computation | async-start | bytes 4194304 | tf_op jit(solution)/shard_map/all_to_all | solution.py:564
  18.1 0.0 copy-done.4
  18.2 0.6 copy.24
  18.8 0.0 copy-done.2
  18.8 0.8 copy.25
  19.6 0.0 copy-done.3
  19.6 0.8 copy.26
  20.4 20.0 %shard_map.191 = (bf16[8,768,384]{2,1,0:T(8,128)(2,1)}, bf16[2,768,384]{2,1,0:T(8,128)(2,1)}, bf16[2,2304,256]{2,1,0:T(8,128)(2,1)}, bf16[2,2304,192]{2,1,0:T(8,128)(2,1)}) custom-call(bf16[9,3,2,24]{3,2,1,0:T(2,128)(2,1)} %bitcast.14, bf16[9,3,24,24]{3,2,1,0:T(8,128)(2,1)} %bitcast.11, bf16[9,3,24,24]{3,2,1,0:T(8,128)(2,1)} %bitcast.12, ...), custom_call_target="tpu_custom_call" | custom-call | flops 20000000000 | bytes 10000000 | tf_op jit(solution)/shard_map/pallas_call | solution.py:358
  40.3 26.7 %all-to-all-done.r_ref = bf16[32,32,1024]{2,1,0:T(8,128)(2,1)S(1)} async-done(((bf16[32,32,1024]{2,1,0:T(8,128)(2,1)}), bf16[32,32,1024]{2,1,0:T(8,128)(2,1)S(1)}, u32[]{:S(2)}, u32[]{:S(2)}) %all-to-all-start) | async-done | bytes 2097184 | tf_op jit(solution)/shard_map/all_to_all | solution.py:564
  67.0 0.0 copy-start
  67.0 1.3 copy-done
  68.4 0.0 copy-start.5
  68.4 0.0 copy-start.6
  68.4 0.0 copy-start.7
  68.4 11.6 %shard_map.192 = bf16[32,24,256]{2,1,0:T(8,128)(2,1)} custom-call(bf16[32,32,1024]{2,1,0:T(8,128)(2,1)} %copy-done, bf16[2,2,1536,256]{3,2,1,0:T(8,128)(2,1)} %constant.39.clone.t_ref, f32[2,8,8,16,512]{4,3,2,1,0:T(8,128)} %refs_1_.1, f32[2,8,8,16,512]{4,3,2,1,0:T(8,128)} %refs_1_.1), custom_call_target="tpu_custom_call" | custom-call | tf_op jit(solution)/shard_map/pallas_call | solution.py:223
  80.0 4.2 %all-to-all-start.1 = ((bf16[32,24,256]{2,1,0:T(8,128)(2,1)}), bf16[32,24,256]{2,1,0:T(8,128)(2,1)S(1)}, u32[]{:S(2)}, u32[]{:S(2)}) async-start(bf16[32,24,256]{2,1,0:T(8,128)(2,1)} %shard_map.192), calls=%async_computation.1 | async-start | bytes 786432 | tf_op jit(solution)/shard_map/all_to_all | solution.py:568
  84.2 0.0 copy-done.5
  84.2 0.1 stack_tile.6
  84.3 0.0 copy-done.6
  84.3 0.1 stack_tile.7
  84.4 0.0 copy-done.7
  84.4 0.1 broadcast_in_dim.3
  84.5 0.7 broadcast_in_dim_reshape.3.b3_ref
  85.2 0.7 pad_add_fusion.place_ref
  85.8 0.6 pad_maximum_fusion.b12_ref
  86.4 10.8 %all-to-all-done.1.in_ref = bf16[32,24,256]{2,1,0:T(8,128)(2,1)S(1)} async-done(((bf16[32,24,256]{2,1,0:T(8,128)(2,1)}), bf16[32,24,256]{2,1,0:T(8,128)(2,1)S(1)}, u32[]{:S(2)}, u32[]{:S(2)}) %all-to-all-start.1) | async-done | bytes 393248 | tf_op jit(solution)/shard_map/all_to_all | solution.py:568
  97.2 0.0 copy-start.1
  97.2 0.7 copy-done.1
  98.0 35.0 %shard_map.193 = bf16[24,16,16,256]{3,2,1,0:T(8,128)(2,1)} custom-call(s32[2]{0:T(128)} %pad_add_fusion.place_ref, bf16[32,24,256]{2,1,0:T(8,128)(2,1)} %copy-done.1, bf16[8,768,384]{2,1,0:T(8,128)(2,1)} %get-tuple-element.19.w1_ref, bf16[2,768,384]{2,1,0:T(8,128)(2,1)} %get-tuple-element.20.w1_side_ref, bf16[2,2304,256]{2,1,0:T(8,128)(2,1)} %get-tuple-element.21.w2_ref, ...), custom_call_target="tpu_custom_call" | custom-call | tf_op jit(solution)/shard_map/pallas_call | solution.py:532
  (2 shorter events, 0.0 us)
Async XLA Ops:
  10.8 7.3 %copy-start.4 = (bf16[24,2,3,3,3]{0,1,4,3,2:T(2,128)(2,1)S(1)}, bf16[24,2,3,3,3]{0,1,4,3,2:T(2,128)(2,1)}, u32[]{:S(2)}) copy-start(bf16[24,2,3,3,3]{0,1,4,3,2:T(2,128)(2,1)} %param.22) | copy-start | bytes 7780
  10.8 8.0 %copy-start.2 = (bf16[24,24,3,3,3]{1,0,4,3,2:T(8,128)(2,1)S(1)}, bf16[24,24,3,3,3]{1,0,4,3,2:T(8,128)(2,1)}, u32[]{:S(2)}) copy-start(bf16[24,24,3,3,3]{1,0,4,3,2:T(8,128)(2,1)} %param.24) | copy-start | bytes 93316
  10.8 8.8 %copy-start.3 = (bf16[24,24,3,3,3]{1,0,4,3,2:T(8,128)(2,1)S(1)}, bf16[24,24,3,3,3]{1,0,4,3,2:T(8,128)(2,1)}, u32[]{:S(2)}) copy-start(bf16[24,24,3,3,3]{1,0,4,3,2:T(8,128)(2,1)} %param.26) | copy-start | bytes 93316
  10.8 56.2 %all-to-all-start = ((bf16[32,32,1024]{2,1,0:T(8,128)(2,1)}), bf16[32,32,1024]{2,1,0:T(8,128)(2,1)S(1)}, u32[]{:S(2)}, u32[]{:S(2)}) async-start(bf16[32,32,1024]{2,1,0:T(8,128)(2,1)} %shard_map.190), calls=%async_computation | async-start | bytes 4194304 | tf_op jit(solution)/shard_map/all_to_all | solution.py:564
  67.0 1.3 copy-start
  68.4 15.9 %copy-start.5 = (f32[24]{0:T(128)S(1)}, f32[24]{0:T(128)}, u32[]{:S(2)}) copy-start(f32[24]{0:T(128)} %param.23) | copy-start | bytes 292
  68.4 16.0 %copy-start.6 = (f32[24]{0:T(128)S(1)}, f32[24]{0:T(128)}, u32[]{:S(2)}) copy-start(f32[24]{0:T(128)} %param.25) | copy-start | bytes 292
  68.4 16.1 %copy-start.7 = (f32[24]{0:T(128)S(1)}, f32[24]{0:T(128)}, u32[]{:S(2)}) copy-start(f32[24]{0:T(128)} %param.27) | copy-start | bytes 292
  80.0 17.2 %all-to-all-start.1 = ((bf16[32,24,256]{2,1,0:T(8,128)(2,1)}), bf16[32,24,256]{2,1,0:T(8,128)(2,1)S(1)}, u32[]{:S(2)}, u32[]{:S(2)}) async-start(bf16[32,24,256]{2,1,0:T(8,128)(2,1)} %shard_map.192), calls=%async_computation.1 | async-start | bytes 786432 | tf_op jit(solution)/shard_map/all_to_all | solution.py:568
  97.2 0.8 copy-start.1

commit v4 on v3

--- a/solution.py
+++ b/solution.py
@@ -80,8 +80,9 @@
 
 def decode(code):
     code = code.astype(F32)
-    root = jnp.sqrt(jnp.sqrt(jnp.abs(code)))
-    return jnp.where(code < 0, -root, root)
+    size = jnp.maximum(jnp.abs(code), 1e-37)
+    inverse = lax.rsqrt(size * lax.rsqrt(size))
+    return code * (inverse * inverse * inverse)
 
 
 def y_kernel(devices, k_ref, t_ref, out_ref, lines, turned, sems):
@@ -163,7 +164,7 @@
         turned[...] = jnp.zeros_like(turned)
 
         def unpack(i, carry):
-            at = pl.ds(pl.multiple_of(i * 32, 32), 32)
+            at = pl.ds(pl.multiple_of(i * 64, 64), 64)
             for parity in range(groups):
                 value = decode(codes[parity, at, :])
                 high = value.astype(BF16)
@@ -171,7 +172,7 @@
                 lines[parity, at, depth:] = (value - high.astype(F32)).astype(BF16)
             return carry
 
-        lax.fori_loop(0, columns // 32, unpack, 0)
+        lax.fori_loop(0, columns // 64, unpack, 0)
 
     products = []
     for parity in range(groups):
@@ -394,10 +395,10 @@
 def net_kernel(
     place_ref,
     in_ref,
-    w1_ref,
-    w1_side_ref,
-    w2_ref,
-    w3_ref,
+    w1_far,
+    w1_side_far,
+    w2_far,
+    w3_far,
     b12_ref,
     b3_ref,
     order_ref,
@@ -408,6 +409,11 @@
     after,
     act1,
     act2,
+    w1_ref,
+    w1_side_ref,
+    w2_ref,
+    w3_ref,
+    sems,
 ):
     devices, rows_in, lanes_in = in_ref.shape
     z1, groups = act1.shape[:2]
@@ -428,8 +434,20 @@
                 pieces.append(piece.reshape(count * y_here * devices, window))
         return jnp.concatenate(pieces, axis=1)
 
+    first_copies = [
+        pltpu.make_async_copy(w1_far.at[m], w1_ref.at[m], sems.at[m]) for m in range(y_here)
+    ]
+    side_copy = pltpu.make_async_copy(w1_side_far, w1_side_ref, sems.at[y_here])
+    second_copy = pltpu.make_async_copy(w2_far, w2_ref, sems.at[y_here + 1])
+    third_copy = pltpu.make_async_copy(w3_far, w3_ref, sems.at[y_here + 2])
+
     @pl.when(pl.program_id(0) == 0)
     def _():
+        side_copy.start()
+        for copy in first_copies:
+            copy.start()
+        second_copy.start()
+        third_copy.start()
         for s in range(devices):
             piece = in_ref[s].astype(F32)
             for j in range(0, lanes_in, 128):
@@ -453,7 +471,9 @@
                 [ref[dz * devices : dz * devices + count, :] for dz in range(3)], axis=1
             )
 
+        side_copy.wait()
         for m in range(y_here):
+            first_copies[m].wait()
             result = jnp.dot(three(own), w1_ref[m], preferred_element_type=F32)
             if m == 0:
                 result += jnp.dot(three(before), w1_side_ref[0], preferred_element_type=F32)
@@ -487,7 +507,9 @@
                 act2[z + i, 0] = down_one(cube[i, y_here - 1]).astype(BF16)
             return carry
 
+        second_copy.wait()
         lax.fori_loop(0, z2 // many, second, 0)
+        third_copy.wait()
         for z in (0, z2 - 1):
             here = first_z + z - 1
 
@@ -533,7 +555,9 @@
         net_kernel,
         out_shape=jax.ShapeDtypeStruct((channels, z_here, xs, y_count), BF16),
         grid=(z_here // THIRD_GROUP,),
-        in_specs=[pl.BlockSpec(memory_space=pltpu.SMEM)] + [vmem_spec()] * 8,
+        in_specs=[pl.BlockSpec(memory_space=pltpu.SMEM), vmem_spec()]
+        + [pl.BlockSpec(memory_space=pl.ANY)] * 4
+        + [vmem_spec()] * 3,
         out_specs=pl.BlockSpec((channels, THIRD_GROUP, xs, y_count), lambda z: (0, z, 0, 0)),
         scratch_shapes=[
             pltpu.VMEM((lanes_in // 128, rows_in * devices, 128), F32),
@@ -542,6 +566,11 @@
             pltpu.VMEM((rows_in * devices, lanes_in), BF16),
             pltpu.VMEM((z1, groups, devices, lanes), BF16),
             pltpu.VMEM((z2, groups, devices, lanes), BF16),
+            pltpu.VMEM(w1.shape, BF16),
+            pltpu.VMEM(w1_side.shape, BF16),
+            pltpu.VMEM(w2.shape, BF16),
+            pltpu.VMEM(w3.shape, BF16),
+            pltpu.SemaphoreType.DMA((y_here + 3,)),
         ],
         compiler_params=params(),
     )(place, gathered, w1, w1_side, w2, w3, b12, b3, order)

time: 133 us -> 130 us (0.977)
  Pallas kernels: 77.3 us -> 74.3 us
    pallas_call x1, Pallas kernels: 11.6 us -> 10 us  [z_transform(): pl.pallas_call(functools.partial(z_kernel, scale, devices, z_count // dev...]
    pallas_call x1, Pallas kernels: 35 us -> 33.5 us  [network(): pl.pallas_call(net_kernel, out_shape=jax.ShapeDtypeStruct((channels, z_he...]
where the time goes in v4:
time: 130 us
  Pallas kernels  74.3 us (57%)
  waiting for transfers between devices  37.5 us (29%)
  starting transfers between devices  11.5 us (9%)
  local copies, waits for them, and re-layouts  5.24 us (4%)
    pallas_call x1, Pallas kernels, network(): pl.pallas_call(net_kernel, out_shape=jax.ShapeDtypeStruct((channels, z_he...  33.5 us
    all_to_all x1, waiting for transfers between devices, on_device(): received = lax.all_to_all(lines, 'kz', 0, 0)  26.7 us
    pallas_call x1, Pallas kernels, expand_weights(): pl.pallas_call(functools.partial(expand_kernel, y_here), out_shape=(jax.S...  20 us
    pallas_call x1, Pallas kernels, y_transform(): pl.pallas_call(functools.partial(y_kernel, devices), out_shape=jax.ShapeD...  10.8 us
    all_to_all x1, waiting for transfers between devices, on_device(): gathered = lax.all_to_all(merged, 'kz', 0, 0)  10.8 us
    pallas_call x1, Pallas kernels, z_transform(): pl.pallas_call(functools.partial(z_kernel, scale, devices, z_count // dev...  10 us
    all_to_all x1, starting transfers between devices, on_device(): received = lax.all_to_all(lines, 'kz', 0, 0)  7.3 us
    all_to_all x1, starting transfers between devices, on_device(): gathered = lax.all_to_all(merged, 'kz', 0, 0)  4.19 us
  transfers between devices with their start and end apart: 2, of which 2 were waited for; matrix products, arithmetic and copies ran while one was open for 3% of the time, Pallas kernels for 15%

profile of v4, /device:TPU:0, one launch (start us, length us, event | category | flops | bytes accessed | tf_op | source)
XLA Modules:
  0.0 130.0 jit_solution(4915677196543122993)
XLA Ops:
  0.0 10.8 %shard_map.190 = bf16[32,32,1024]{2,1,0:T(8,128)(2,1)} custom-call(f32[128,16,512]{2,1,0:T(8,128)} %bitcast.8, bf16[512,1536]{1,0:T(8,128)(2,1)} %constant.30.clone.t_ref), custom_call_target="tpu_custom_call" | custom-call | tf_op jit(solution)/shard_map/pallas_call | solution.py:136
  10.8 0.0 copy-start.4
  10.8 0.0 copy-start.2
  10.8 0.0 copy-start.3
  10.8 7.3 %all-to-all-start = ((bf16[32,32,1024]{2,1,0:T(8,128)(2,1)}), bf16[32,32,1024]{2,1,0:T(8,128)(2,1)S(1)}, u32[]{:S(2)}, u32[]{:S(2)}) async-start(bf16[32,32,1024]{2,1,0:T(8,128)(2,1)} %shard_map.190), calls=%async_computation | async-start | bytes 4194304 | tf_op jit(solution)/shard_map/all_to_all | solution.py:593
  18.1 0.0 copy-done.4
  18.2 0.6 copy.24
  18.8 0.0 copy-done.2
  18.8 0.8 copy.25
  19.6 0.0 copy-done.3
  19.6 0.8 copy.26
  20.4 20.0 %shard_map.191 = (bf16[8,768,384]{2,1,0:T(8,128)(2,1)}, bf16[2,768,384]{2,1,0:T(8,128)(2,1)}, bf16[2,2304,256]{2,1,0:T(8,128)(2,1)}, bf16[2,2304,192]{2,1,0:T(8,128)(2,1)}) custom-call(bf16[9,3,2,24]{3,2,1,0:T(2,128)(2,1)} %bitcast.14, bf16[9,3,24,24]{3,2,1,0:T(8,128)(2,1)} %bitcast.11, bf16[9,3,24,24]{3,2,1,0:T(8,128)(2,1)} %bitcast.12, ...), custom_call_target="tpu_custom_call" | custom-call | flops 20000000000 | bytes 10000000 | tf_op jit(solution)/shard_map/pallas_call | solution.py:359
  40.3 26.7 %all-to-all-done.r_ref = bf16[32,32,1024]{2,1,0:T(8,128)(2,1)S(1)} async-done(((bf16[32,32,1024]{2,1,0:T(8,128)(2,1)}), bf16[32,32,1024]{2,1,0:T(8,128)(2,1)S(1)}, u32[]{:S(2)}, u32[]{:S(2)}) %all-to-all-start) | async-done | bytes 2097184 | tf_op jit(solution)/shard_map/all_to_all | solution.py:593
  67.0 0.0 copy-start
  67.0 1.3 %copy-done = bf16[32,32,1024]{2,1,0:T(8,128)(2,1)} copy-done((bf16[32,32,1024]{2,1,0:T(8,128)(2,1)}, bf16[32,32,1024]{2,1,0:T(8,128)(2,1)S(1)}, u32[]{:S(2)}) %copy-start) | copy-done | bytes 2097176
  68.4 0.0 copy-start.5
  68.4 0.0 copy-start.6
  68.4 0.0 copy-start.7
  68.4 10.0 %shard_map.192 = bf16[32,24,256]{2,1,0:T(8,128)(2,1)} custom-call(bf16[32,32,1024]{2,1,0:T(8,128)(2,1)} %copy-done, bf16[2,2,1536,256]{3,2,1,0:T(8,128)(2,1)} %constant.39.clone.t_ref, f32[2,8,8,16,512]{4,3,2,1,0:T(8,128)} %refs_1_.1, f32[2,8,8,16,512]{4,3,2,1,0:T(8,128)} %refs_1_.1), custom_call_target="tpu_custom_call" | custom-call | tf_op jit(solution)/shard_map/pallas_call | solution.py:224
  78.4 4.2 %all-to-all-start.1 = ((bf16[32,24,256]{2,1,0:T(8,128)(2,1)}), bf16[32,24,256]{2,1,0:T(8,128)(2,1)S(1)}, u32[]{:S(2)}, u32[]{:S(2)}) async-start(bf16[32,24,256]{2,1,0:T(8,128)(2,1)} %shard_map.192), calls=%async_computation.1 | async-start | bytes 786432 | tf_op jit(solution)/shard_map/all_to_all | solution.py:597
  82.6 0.0 copy-done.5
  82.6 0.1 stack_tile.6
  82.7 0.0 copy-done.6
  82.7 0.1 stack_tile.7
  82.8 0.0 copy-done.7
  82.8 0.1 broadcast_in_dim.3
  82.9 0.7 broadcast_in_dim_reshape.3.b3_ref
  83.6 0.7 pad_add_fusion.place_ref
  84.3 0.6 pad_maximum_fusion.b12_ref
  84.8 10.8 %all-to-all-done.1.in_ref = bf16[32,24,256]{2,1,0:T(8,128)(2,1)S(1)} async-done(((bf16[32,24,256]{2,1,0:T(8,128)(2,1)}), bf16[32,24,256]{2,1,0:T(8,128)(2,1)S(1)}, u32[]{:S(2)}, u32[]{:S(2)}) %all-to-all-start.1) | async-done | bytes 393248 | tf_op jit(solution)/shard_map/all_to_all | solution.py:597
  95.6 0.0 copy-start.1
  95.6 0.7 copy-done.1
  96.4 33.5 %shard_map.193 = bf16[24,16,16,256]{3,2,1,0:T(8,128)(2,1)} custom-call(s32[2]{0:T(128)} %pad_add_fusion.place_ref, bf16[32,24,256]{2,1,0:T(8,128)(2,1)} %copy-done.1, bf16[8,768,384]{2,1,0:T(8,128)(2,1)} %get-tuple-element.19.w1_far, bf16[2,768,384]{2,1,0:T(8,128)(2,1)} %get-tuple-element.20.w1_side_far, bf16[2,2304,256]{2,1,0:T(8,128)(2,1)} %get-tuple-element.21.w2_far, ...), custom_call_target="tpu_custom_call" | custom-call | tf_op jit(solution)/shard_map/pallas_call | solution.py:554
  (2 shorter events, 0.0 us)
Async XLA Ops:
  10.8 7.3 %copy-start.4 = (bf16[24,2,3,3,3]{0,1,4,3,2:T(2,128)(2,1)S(1)}, bf16[24,2,3,3,3]{0,1,4,3,2:T(2,128)(2,1)}, u32[]{:S(2)}) copy-start(bf16[24,2,3,3,3]{0,1,4,3,2:T(2,128)(2,1)} %param.22) | copy-start | bytes 7780
  10.8 8.0 %copy-start.2 = (bf16[24,24,3,3,3]{1,0,4,3,2:T(8,128)(2,1)S(1)}, bf16[24,24,3,3,3]{1,0,4,3,2:T(8,128)(2,1)}, u32[]{:S(2)}) copy-start(bf16[24,24,3,3,3]{1,0,4,3,2:T(8,128)(2,1)} %param.24) | copy-start | bytes 93316
  10.8 8.8 %copy-start.3 = (bf16[24,24,3,3,3]{1,0,4,3,2:T(8,128)(2,1)S(1)}, bf16[24,24,3,3,3]{1,0,4,3,2:T(8,128)(2,1)}, u32[]{:S(2)}) copy-start(bf16[24,24,3,3,3]{1,0,4,3,2:T(8,128)(2,1)} %param.26) | copy-start | bytes 93316
  10.8 56.2 %all-to-all-start = ((bf16[32,32,1024]{2,1,0:T(8,128)(2,1)}), bf16[32,32,1024]{2,1,0:T(8,128)(2,1)S(1)}, u32[]{:S(2)}, u32[]{:S(2)}) async-start(bf16[32,32,1024]{2,1,0:T(8,128)(2,1)} %shard_map.190), calls=%async_computation | async-start | bytes 4194304 | tf_op jit(solution)/shard_map/all_to_all | solution.py:593
  67.0 1.3 %copy-start = (bf16[32,32,1024]{2,1,0:T(8,128)(2,1)}, bf16[32,32,1024]{2,1,0:T(8,128)(2,1)S(1)}, u32[]{:S(2)}) copy-start(bf16[32,32,1024]{2,1,0:T(8,128)(2,1)S(1)} %all-to-all-done.r_ref) | copy-start | bytes 6291460
  68.4 14.3 %copy-start.5 = (f32[24]{0:T(128)S(1)}, f32[24]{0:T(128)}, u32[]{:S(2)}) copy-start(f32[24]{0:T(128)} %param.23) | copy-start | bytes 292
  68.4 14.4 %copy-start.6 = (f32[24]{0:T(128)S(1)}, f32[24]{0:T(128)}, u32[]{:S(2)}) copy-start(f32[24]{0:T(128)} %param.25) | copy-start | bytes 292
  68.4 14.5 %copy-start.7 = (f32[24]{0:T(128)S(1)}, f32[24]{0:T(128)}, u32[]{:S(2)}) copy-start(f32[24]{0:T(128)} %param.27) | copy-start | bytes 292
  78.4 17.2 %all-to-all-start.1 = ((bf16[32,24,256]{2,1,0:T(8,128)(2,1)}), bf16[32,24,256]{2,1,0:T(8,128)(2,1)S(1)}, u32[]{:S(2)}, u32[]{:S(2)}) async-start(bf16[32,24,256]{2,1,0:T(8,128)(2,1)} %shard_map.192), calls=%async_computation.1 | async-start | bytes 786432 | tf_op jit(solution)/shard_map/all_to_all | solution.py:597
  95.6 0.8 copy-start.1

commit v5 on v4

--- a/solution.py
+++ b/solution.py
@@ -17,8 +17,8 @@
 Y_PASSES = 3
 Z_WIDTH = 128
 CODE_SCALE = 2.0**20
-SECOND_GROUP = 3
-THIRD_GROUP = 4
+SECOND_GROUP = 6
+THIRD_GROUP = 8
 VMEM_LIMIT = 56 * 1024 * 1024
 
 
@@ -147,60 +147,83 @@
     )(kspace.reshape(pairs, kz_here, width), table)
 
 
-def z_kernel(scale, devices, z_here, groups, r_ref, t_ref, *refs):
-    s_refs, out_ref, codes, lines, turned = refs[:groups], *refs[groups:]
-    step = pl.program_id(0)
-    _, y_here, coils, xs, width = s_refs[0].shape
+def z_kernel(
+    scale, z_here, groups, r_ref, t_far, s_far, out_ref, codes, lines, turned, t_ref, s_ref, sems
+):
+    devices = r_ref.shape[0]
+    steps, _, _, y_here, coils, xs, width = s_ref.shape
     lanes = out_ref.shape[2]
     columns = r_ref.shape[2]
     rows = r_ref.shape[1] // groups
     depth = devices * rows
-
-    @pl.when(step == 0)
-    def _():
+    copies = []
+    for step in range(steps):
+        found = [
+            pltpu.make_async_copy(
+                t_far.at[:, step], t_ref.at[:, step], sems.at[step * (groups + 1) + groups]
+            )
+        ]
+        for part in range(groups):
+            z = pl.ds((part * steps + step) * width, width)
+            found.append(
+                pltpu.make_async_copy(
+                    s_far.at[:, :, :, :, z],
+                    s_ref.at[step, part],
+                    sems.at[step * (groups + 1) + part],
+                )
+            )
+        copies.append(found)
+    for found in copies:
+        for copy in found:
+            copy.start()
+    for parity in range(groups):
+        piece = r_ref[:, parity * rows : (parity + 1) * rows, :]
+        codes[parity] = piece.reshape(depth, columns).T
+    turned[...] = jnp.zeros_like(turned)
+
+    def unpack(i, carry):
+        at = pl.ds(pl.multiple_of(i * 64, 64), 64)
         for parity in range(groups):
-            piece = r_ref[:, parity * rows : (parity + 1) * rows, :]
-            codes[parity] = piece.reshape(depth, columns).T
-        turned[...] = jnp.zeros_like(turned)
-
-        def unpack(i, carry):
-            at = pl.ds(pl.multiple_of(i * 64, 64), 64)
-            for parity in range(groups):
-                value = decode(codes[parity, at, :])
-                high = value.astype(BF16)
-                lines[parity, at, :depth] = high
-                lines[parity, at, depth:] = (value - high.astype(F32)).astype(BF16)
-            return carry
-
-        lax.fori_loop(0, columns // 64, unpack, 0)
-
+            value = decode(codes[parity, at, :])
+            high = value.astype(BF16)
+            lines[parity, at, :depth] = high
+            lines[parity, at, depth:] = (value - high.astype(F32)).astype(BF16)
+        return carry
+
+    lax.fori_loop(0, columns // 64, unpack, 0)
+    for step in range(steps):
+        for copy in copies[step]:
+            copy.wait()
+        z_step(scale, groups, step, lines, t_ref, s_ref, turned)
+    for device in range(devices):
+        first = 8 + device * z_here - HALO
+        out_ref[device] = turned[first : first + out_ref.shape[1], :].astype(BF16)
+
+
+def z_step(scale, groups, step, lines, t_ref, s_ref, turned):
+    steps, _, _, y_here, coils, xs, width = s_ref.shape
+    depth = lines.shape[2] // 2
+    lanes = turned.shape[1]
     products = []
     for parity in range(groups):
         operand = lines[parity]
         operand = jnp.concatenate([operand, operand[:, :depth]], axis=1)
-        products.append(jnp.dot(operand, t_ref[parity, 0], preferred_element_type=F32))
+        products.append(jnp.dot(operand, t_ref[parity, step], preferred_element_type=F32))
     if groups == 2:
         products = [products[0] + products[1], products[0] - products[1]]
-    for part, (images, s_ref) in enumerate(zip(products, s_refs)):
+    for part, images in enumerate(products):
         image_re = images[:, :width].reshape(y_here, coils, xs, width)
         image_im = images[:, width:].reshape(y_here, coils, xs, width)
-        sens_re = s_ref[0]
-        sens_im = s_ref[1]
+        sens_re = s_ref[step, part, 0]
+        sens_im = s_ref[step, part, 1]
         real = jnp.sum(sens_re * image_re + sens_im * image_im, axis=1) * scale
         imag = jnp.sum(sens_re * image_im - sens_im * image_re, axis=1) * scale
         merged = jnp.concatenate([real, imag], axis=1).reshape(y_here * 2 * xs, width)
         extra = lanes - y_here * 2 * xs
         if extra:
             merged = jnp.concatenate([merged, jnp.zeros((extra, width), F32)], axis=0)
-        base = 8 + part * devices * z_here // groups
-        base = pl.multiple_of(base + step * width, 8)
-        turned[pl.ds(base, width), :] = merged.T
-
-    @pl.when(step == pl.num_programs(0) - 1)
-    def _():
-        for device in range(devices):
-            first = 8 + device * z_here - HALO
-            out_ref[device] = turned[first : first + out_ref.shape[1], :].astype(BF16)
+        base = 8 + (part * steps + step) * width
+        turned[base : base + width, :] = merged.T
 
 
 def z_transform(received, sensitivity, devices):
@@ -216,28 +239,21 @@
     steps = z_count // groups // width
     depth = 2 * z_count // groups
 
-    def sens_spec(part):
-        return pl.BlockSpec(
-            (2, y_here, coils, xs, width), lambda z: (0, 0, 0, 0, z + part * steps)
-        )
-
     return pl.pallas_call(
-        functools.partial(z_kernel, scale, devices, z_count // devices, groups),
+        functools.partial(z_kernel, scale, z_count // devices, groups),
         out_shape=jax.ShapeDtypeStruct((devices, rows, lanes), BF16),
-        grid=(steps,),
-        in_specs=[
-            pl.BlockSpec(received.shape, lambda z: (0, 0, 0)),
-            pl.BlockSpec((groups, 1, 3 * depth, 2 * width), lambda z: (0, z, 0, 0)),
-        ]
-        + [sens_spec(part) for part in range(groups)],
-        out_specs=pl.BlockSpec((devices, rows, lanes), lambda z: (0, 0, 0)),
+        in_specs=[vmem_spec()] + [pl.BlockSpec(memory_space=pl.ANY)] * 2,
+        out_specs=vmem_spec(),
         scratch_shapes=[
             pltpu.VMEM((groups, y_here * pairs, depth), BF16),
             pltpu.VMEM((groups, y_here * pairs, 2 * depth), BF16),
             pltpu.VMEM((8 + z_count + 32, lanes), F32),
+            pltpu.VMEM(table.shape, BF16),
+            pltpu.VMEM((steps, groups, 2, y_here, coils, xs, width), F32),
+            pltpu.SemaphoreType.DMA((steps * (groups + 1),)),
         ],
         compiler_params=params(),
-    )(received, table, *[sensitivity] * groups)
+    )(received, table, sensitivity)
 
 
 def window_starts(lanes):
@@ -493,7 +509,7 @@
             def _():
                 act1[z] = jnp.zeros_like(act1[z])
 
-        many = SECOND_GROUP
+        many = min(SECOND_GROUP, z2)
 
         def second(step, carry):
             z = step * many
@@ -550,15 +566,16 @@
     order[row, row % devices * y_here + row // devices] = 1.0
     order = jnp.asarray(order, BF16)
     z1, z2 = z_here + 4, z_here + 2
+    step = min(THIRD_GROUP, z_here)
     groups = y_here + 2
     return pl.pallas_call(
         net_kernel,
         out_shape=jax.ShapeDtypeStruct((channels, z_here, xs, y_count), BF16),
-        grid=(z_here // THIRD_GROUP,),
+        grid=(z_here // step,),
         in_specs=[pl.BlockSpec(memory_space=pltpu.SMEM), vmem_spec()]
         + [pl.BlockSpec(memory_space=pl.ANY)] * 4
         + [vmem_spec()] * 3,
-        out_specs=pl.BlockSpec((channels, THIRD_GROUP, xs, y_count), lambda z: (0, z, 0, 0)),
+        out_specs=pl.BlockSpec((channels, step, xs, y_count), lambda z: (0, z, 0, 0)),
         scratch_shapes=[
             pltpu.VMEM((lanes_in // 128, rows_in * devices, 128), F32),
             pltpu.VMEM((rows_in * devices, lanes_in), BF16),

time: 130 us -> 129 us (level)
  Pallas kernels: 74.3 us -> 72.4 us
  transfers between devices with their start and end apart: 2 -> 2, of which waited for: 2 -> 2; matrix products, arithmetic and copies ran while one was open for 3% -> 3% of each run, Pallas kernels for 15% -> 16%
where the time goes in v5:
time: 129 us; the launch traced here: 128 us
  Pallas kernels  72.4 us (56%)
  waiting for transfers between devices  37.7 us (29%)
  starting transfers between devices  11.3 us (9%)
  local copies, waits for them, and re-layouts  5.24 us (4%)
    pallas_call x1, Pallas kernels, network(): pl.pallas_call(net_kernel, out_shape=jax.ShapeDtypeStruct((channels, z_he...  32.8 us
    all_to_all x1, waiting for transfers between devices, on_device(): received = lax.all_to_all(lines, 'kz', 0, 0)  26.7 us
    pallas_call x1, Pallas kernels, expand_weights(): pl.pallas_call(functools.partial(expand_kernel, y_here), out_shape=(jax.S...  20 us
    all_to_all x1, waiting for transfers between devices, on_device(): gathered = lax.all_to_all(merged, 'kz', 0, 0)  10.9 us
    pallas_call x1, Pallas kernels, y_transform(): pl.pallas_call(functools.partial(y_kernel, devices), out_shape=jax.ShapeD...  10.8 us
    pallas_call x1, Pallas kernels, z_transform(): pl.pallas_call(functools.partial(z_kernel, scale, z_count // devices, gro...  8.85 us
    all_to_all x1, starting transfers between devices, on_device(): received = lax.all_to_all(lines, 'kz', 0, 0)  7.3 us
    all_to_all x1, starting transfers between devices, on_device(): gathered = lax.all_to_all(merged, 'kz', 0, 0)  4.02 us
  transfers between devices with their start and end apart: 2, of which 2 were waited for; matrix products, arithmetic and copies ran while one was open for 3% of the time, Pallas kernels for 16%

profile of v5, /device:TPU:0, one launch (start us, length us, event | category | flops | bytes accessed | tf_op | source)
XLA Modules:
  0.0 128.2 jit_solution(16825434254817638370)
XLA Ops:
  0.0 10.8 %shard_map.190 = bf16[32,32,1024]{2,1,0:T(8,128)(2,1)} custom-call(f32[128,16,512]{2,1,0:T(8,128)} %bitcast.8, bf16[512,1536]{1,0:T(8,128)(2,1)} %constant.30.clone.t_ref), custom_call_target="tpu_custom_call" | custom-call | tf_op jit(solution)/shard_map/pallas_call | solution.py:136
  10.8 0.0 copy-start.4
  10.8 0.0 copy-start.2
  10.8 0.0 copy-start.3
  10.8 7.3 %all-to-all-start = ((bf16[32,32,1024]{2,1,0:T(8,128)(2,1)}), bf16[32,32,1024]{2,1,0:T(8,128)(2,1)S(1)}, u32[]{:S(2)}, u32[]{:S(2)}) async-start(bf16[32,32,1024]{2,1,0:T(8,128)(2,1)} %shard_map.190), calls=%async_computation | async-start | bytes 4194304 | tf_op jit(solution)/shard_map/all_to_all | solution.py:610
  18.1 0.0 copy-done.4
  18.2 0.6 copy.24
  18.8 0.0 copy-done.2
  18.8 0.8 copy.25
  19.6 0.0 copy-done.3
  19.6 0.8 copy.26
  20.4 20.0 %shard_map.191 = (bf16[8,768,384]{2,1,0:T(8,128)(2,1)}, bf16[2,768,384]{2,1,0:T(8,128)(2,1)}, bf16[2,2304,256]{2,1,0:T(8,128)(2,1)}, bf16[2,2304,192]{2,1,0:T(8,128)(2,1)}) custom-call(bf16[9,3,2,24]{3,2,1,0:T(2,128)(2,1)} %bitcast.14, bf16[9,3,24,24]{3,2,1,0:T(8,128)(2,1)} %bitcast.11, bf16[9,3,24,24]{3,2,1,0:T(8,128)(2,1)} %bitcast.12, ...), custom_call_target="tpu_custom_call" | custom-call | flops 20000000000 | bytes 10000000 | tf_op jit(solution)/shard_map/pallas_call | solution.py:375
  40.3 26.7 %all-to-all-done.r_ref = bf16[32,32,1024]{2,1,0:T(8,128)(2,1)S(1)} async-done(((bf16[32,32,1024]{2,1,0:T(8,128)(2,1)}), bf16[32,32,1024]{2,1,0:T(8,128)(2,1)S(1)}, u32[]{:S(2)}, u32[]{:S(2)}) %all-to-all-start) | async-done | bytes 2097184 | tf_op jit(solution)/shard_map/all_to_all | solution.py:610
  67.0 0.0 copy-start
  67.0 1.3 %copy-done = bf16[32,32,1024]{2,1,0:T(8,128)(2,1)} copy-done((bf16[32,32,1024]{2,1,0:T(8,128)(2,1)}, bf16[32,32,1024]{2,1,0:T(8,128)(2,1)S(1)}, u32[]{:S(2)}) %copy-start) | copy-done | bytes 2097176
  68.4 0.0 copy-start.5
  68.4 0.0 copy-start.6
  68.4 0.0 copy-start.7
  68.4 8.9 %shard_map.192 = bf16[32,24,256]{2,1,0:T(8,128)(2,1)} custom-call(bf16[32,32,1024]{2,1,0:T(8,128)(2,1)} %copy-done, bf16[2,2,1536,256]{3,2,1,0:T(8,128)(2,1)} %constant.39.clone.t_far, f32[2,8,8,16,512]{4,3,2,1,0:T(8,128)} %s_far.1), custom_call_target="tpu_custom_call" | custom-call | tf_op jit(solution)/shard_map/pallas_call | solution.py:242
  77.2 4.0 %all-to-all-start.1 = ((bf16[32,24,256]{2,1,0:T(8,128)(2,1)}), bf16[32,24,256]{2,1,0:T(8,128)(2,1)S(1)}, u32[]{:S(2)}, u32[]{:S(2)}) async-start(bf16[32,24,256]{2,1,0:T(8,128)(2,1)} %shard_map.192), calls=%async_computation.1 | async-start | bytes 786432 | tf_op jit(solution)/shard_map/all_to_all | solution.py:614
  81.3 0.0 copy-done.5
  81.3 0.1 stack_tile.6
  81.4 0.0 copy-done.6
  81.4 0.1 stack_tile.7
  81.5 0.0 copy-done.7
  81.5 0.1 broadcast_in_dim.3
  81.6 0.7 broadcast_in_dim_reshape.3.b3_ref
  82.2 0.7 pad_add_fusion.place_ref
  82.9 0.6 pad_maximum_fusion.b12_ref
  83.5 10.9 %all-to-all-done.1.in_ref = bf16[32,24,256]{2,1,0:T(8,128)(2,1)S(1)} async-done(((bf16[32,24,256]{2,1,0:T(8,128)(2,1)}), bf16[32,24,256]{2,1,0:T(8,128)(2,1)S(1)}, u32[]{:S(2)}, u32[]{:S(2)}) %all-to-all-start.1) | async-done | bytes 393248 | tf_op jit(solution)/shard_map/all_to_all | solution.py:614
  94.4 0.0 copy-start.1
  94.4 0.7 copy-done.1
  95.2 32.8 %shard_map.193 = bf16[24,16,16,256]{3,2,1,0:T(8,128)(2,1)} custom-call(s32[2]{0:T(128)} %pad_add_fusion.place_ref, bf16[32,24,256]{2,1,0:T(8,128)(2,1)} %copy-done.1, bf16[8,768,384]{2,1,0:T(8,128)(2,1)} %get-tuple-element.19.w1_far, bf16[2,768,384]{2,1,0:T(8,128)(2,1)} %get-tuple-element.20.w1_side_far, bf16[2,2304,256]{2,1,0:T(8,128)(2,1)} %get-tuple-element.21.w2_far, ...), custom_call_target="tpu_custom_call" | custom-call | tf_op jit(solution)/shard_map/pallas_call | solution.py:571
  (2 shorter events, 0.0 us)
Async XLA Ops:
  10.8 7.3 %copy-start.4 = (bf16[24,2,3,3,3]{0,1,4,3,2:T(2,128)(2,1)S(1)}, bf16[24,2,3,3,3]{0,1,4,3,2:T(2,128)(2,1)}, u32[]{:S(2)}) copy-start(bf16[24,2,3,3,3]{0,1,4,3,2:T(2,128)(2,1)} %param.22) | copy-start | bytes 7780
  10.8 8.0 %copy-start.2 = (bf16[24,24,3,3,3]{1,0,4,3,2:T(8,128)(2,1)S(1)}, bf16[24,24,3,3,3]{1,0,4,3,2:T(8,128)(2,1)}, u32[]{:S(2)}) copy-start(bf16[24,24,3,3,3]{1,0,4,3,2:T(8,128)(2,1)} %param.24) | copy-start | bytes 93316
  10.8 8.8 %copy-start.3 = (bf16[24,24,3,3,3]{1,0,4,3,2:T(8,128)(2,1)S(1)}, bf16[24,24,3,3,3]{1,0,4,3,2:T(8,128)(2,1)}, u32[]{:S(2)}) copy-start(bf16[24,24,3,3,3]{1,0,4,3,2:T(8,128)(2,1)} %param.26) | copy-start | bytes 93316
  10.8 56.2 %all-to-all-start = ((bf16[32,32,1024]{2,1,0:T(8,128)(2,1)}), bf16[32,32,1024]{2,1,0:T(8,128)(2,1)S(1)}, u32[]{:S(2)}, u32[]{:S(2)}) async-start(bf16[32,32,1024]{2,1,0:T(8,128)(2,1)} %shard_map.190), calls=%async_computation | async-start | bytes 4194304 | tf_op jit(solution)/shard_map/all_to_all | solution.py:610
  67.0 1.3 %copy-start = (bf16[32,32,1024]{2,1,0:T(8,128)(2,1)}, bf16[32,32,1024]{2,1,0:T(8,128)(2,1)S(1)}, u32[]{:S(2)}) copy-start(bf16[32,32,1024]{2,1,0:T(8,128)(2,1)S(1)} %all-to-all-done.r_ref) | copy-start | bytes 6291460
  68.4 12.9 %copy-start.5 = (f32[24]{0:T(128)S(1)}, f32[24]{0:T(128)}, u32[]{:S(2)}) copy-start(f32[24]{0:T(128)} %param.23) | copy-start | bytes 292
  68.4 13.0 %copy-start.6 = (f32[24]{0:T(128)S(1)}, f32[24]{0:T(128)}, u32[]{:S(2)}) copy-start(f32[24]{0:T(128)} %param.25) | copy-start | bytes 292
  68.4 13.1 %copy-start.7 = (f32[24]{0:T(128)S(1)}, f32[24]{0:T(128)}, u32[]{:S(2)}) copy-start(f32[24]{0:T(128)} %param.27) | copy-start | bytes 292
  77.2 17.2 %all-to-all-start.1 = ((bf16[32,24,256]{2,1,0:T(8,128)(2,1)}), bf16[32,24,256]{2,1,0:T(8,128)(2,1)S(1)}, u32[]{:S(2)}, u32[]{:S(2)}) async-start(bf16[32,24,256]{2,1,0:T(8,128)(2,1)} %shard_map.192), calls=%async_computation.1 | async-start | bytes 786432 | tf_op jit(solution)/shard_map/all_to_all | solution.py:614
  94.4 0.8 copy-start.1
